TPU v7x, 32 devices: a whole 2x2x4 slice. The times are simulated.
32 devices in a mesh: ctx: 8 (over y, x, core), head: 4 (over z).
Axes of the slice: x: 2, y: 2, z: 4, core: 2. Of those that a mesh axis runs over, the one named last changes fastest.
Arguments:
- query_proj: bfloat16 [4096, 2048], P('ctx', 'head'), may hold values from -32 to 32
- projected_keys: bfloat16 [4096, 1024], P('ctx', 'head'), may hold values from -32 to 32
- projected_values: bfloat16 [4096, 1024], P('ctx', 'head'), may hold values from -12 to 12
- w_out: bfloat16 [2048, 4096], P('head'), may hold values from -0.1875 to 0.1875
- attended_blocks: int32 [8, 8], replicated, may hold values from -1 to 7, as said below
- grad_out: bfloat16 [4096, 4096], P('ctx', 'head'), may hold values from -6 to 6
Outputs:
- layer_out: bfloat16 [4096, 4096], P('ctx', 'head')
- grad_query: float32 [4096, 2048], P('ctx', 'head')
- grad_key: float32 [4096, 1024], P('ctx', 'head')
- grad_value: float32 [4096, 1024], P('ctx', 'head')
- grad_wout: float32 [2048, 4096], P('head', 'ctx')
Inputs may be any that keep to these rules, and one draw needn't show every extreme that they name: `attended_blocks`: row b lists key blocks: its first entry is b; if b >= 4 its second entry is b - 4; the other live entries are distinct blocks among b - 7 to b - 1; -1 fills the unused entries. Row b has between min(2, b + 1) and 8 live entries, and some row has exactly 8.
All inputs are finite; a program needn't handle non-finite values.
Results may differ from a plain program's by a relative error of at most 0.04.
Values may be sent and summed in bfloat16 or wider, within the bound.
A program may use at most 128 MiB of HBM per device.

v0:
```python
import jax
import jax.numpy as jnp
from jax import lax
from jax.sharding import PartitionSpec as P

HEAD_SIZE = 128
BLOCK_TOKENS = 512


def shifted(value, axis, steps):
    count = lax.axis_size(axis)
    leading, last = (max(0, -steps), min(count, count - steps))
    return lax.ppermute(value, axis, [(source, source + steps) for source in range(leading, last)])


def load_key_block(source, local_index, kv_heads):
    rows_per_block = lax.dynamic_slice_in_dim(source, local_index * BLOCK_TOKENS, BLOCK_TOKENS, 0)
    return rows_per_block.reshape(BLOCK_TOKENS, kv_heads, HEAD_SIZE)


def causal_scores(query_portion, key_row_slice, key_block_index, diagonal_block):
    raw_scores = jnp.einsum(
        "ikgd,jkd->kgij", query_portion, key_row_slice, preferred_element_type=jnp.float32
    ) * HEAD_SIZE ** (-0.5)
    row_pos = lax.broadcasted_iota(jnp.int32, (BLOCK_TOKENS, BLOCK_TOKENS), 0)
    col_pos = lax.broadcasted_iota(jnp.int32, (BLOCK_TOKENS, BLOCK_TOKENS), 1)
    allowed = (key_block_index < diagonal_block) | (col_pos <= row_pos)
    return jnp.where(allowed, raw_scores, -jnp.inf)


def per_device(query_proj, projected_keys, projected_values, w_out, attended_blocks, grad_out):
    ctx_rank = lax.axis_index("ctx")
    ctx_count = lax.axis_size("ctx")
    local_rows = query_proj.shape[0]
    blocks_here = local_rows // BLOCK_TOKENS
    kv_heads = projected_keys.shape[1] // HEAD_SIZE
    key_column_span = projected_keys.shape[1]
    head_cols = query_proj.shape[1]
    heads_per_group = head_cols // HEAD_SIZE // kv_heads
    slot_count = attended_blocks.shape[1]
    score_scale = HEAD_SIZE ** (-0.5)
    reach = min((slot_count - 1 + blocks_here - 1) // blocks_here, ctx_count - 1)
    margin_rows = reach * local_rows
    far_step = ctx_count // 2
    use_far = far_step > reach
    window_rows = margin_rows + local_rows
    front_rows = max(reach, far_step) * local_rows
    all_keys, all_values = (
        lax.all_gather(projected_keys, "ctx", axis=0, tiled=True),
        lax.all_gather(projected_values, "ctx", axis=0, tiled=True),
    )
    total_rows = all_keys.shape[0]

    def heads_of(source):
        return source.reshape(BLOCK_TOKENS, kv_heads, heads_per_group, HEAD_SIZE)

    local_block = 0
    diagonal_block = ctx_rank * blocks_here + local_block
    listed = lax.dynamic_index_in_dim(attended_blocks, diagonal_block, 0, keepdims=False)
    query_portion = heads_of(query_proj)

    def forward_visit(slot_num, running):
        key_block_index = listed[slot_num]

        def forward_live(present_block):
            running_largest, softmax_denominator, weighted_values = present_block
            score_matrix = causal_scores(
                query_portion,
                load_key_block(all_keys, key_block_index, kv_heads),
                key_block_index,
                diagonal_block,
            )
            new_largest = jnp.maximum(running_largest, jnp.max(score_matrix, -1))
            rescale = jnp.exp(running_largest - new_largest)
            attention_weights = jnp.exp(score_matrix - new_largest[..., None])
            softmax_denominator = softmax_denominator * rescale + jnp.sum(attention_weights, -1)
            value_row_slice = load_key_block(all_values, key_block_index, kv_heads)
            weighted_values = weighted_values * rescale[..., None] + jnp.einsum(
                "mayf,fmb->mayb",
                attention_weights.astype(jnp.bfloat16),
                value_row_slice,
                preferred_element_type=jnp.float32,
            )
            return (new_largest, softmax_denominator, weighted_values)

        return lax.cond(
            key_block_index >= 0, forward_live, lambda present_block: present_block, running
        )

    initial_state = (
        jnp.full((kv_heads, heads_per_group, BLOCK_TOKENS), -jnp.inf, jnp.float32),
        jnp.zeros((kv_heads, heads_per_group, BLOCK_TOKENS), jnp.float32),
        jnp.zeros((kv_heads, heads_per_group, BLOCK_TOKENS, HEAD_SIZE), jnp.float32),
    )
    running_largest, softmax_denominator, weighted_values = lax.fori_loop(
        0, slot_count, forward_visit, initial_state
    )
    attn_block = (weighted_values / softmax_denominator[..., None]).astype(jnp.bfloat16)
    attn_parts = attn_block.transpose(2, 0, 1, 3).reshape(BLOCK_TOKENS, head_cols)
    log_totals = [running_largest + jnp.log(softmax_denominator)]
    out_terms = jnp.dot(attn_parts, w_out, preferred_element_type=jnp.float32)
    layer_out = lax.psum_scatter(
        out_terms.astype(jnp.bfloat16), "head", scatter_dimension=1, tiled=True
    )
    piece = lax.all_gather(grad_out, "head", axis=1, tiled=True)
    grad_sum = lax.dot_general(
        piece, w_out, (((1,), (1,)), ((), ())), preferred_element_type=jnp.float32
    )
    column_term = lax.dot_general(
        attn_parts, piece, (((0,), (0,)), ((), ())), preferred_element_type=jnp.float32
    )
    weight_terms = column_term
    grad_sum, weight_terms = (grad_sum, weight_terms)
    grad_attn = grad_sum.astype(jnp.bfloat16)
    grad_wout = lax.psum_scatter(
        weight_terms.astype(jnp.bfloat16), "ctx", scatter_dimension=1, tiled=True
    ).astype(jnp.float32)
    key_gradient_totals = jnp.zeros((total_rows, key_column_span), jnp.float32)
    value_gradient_totals = jnp.zeros((total_rows, key_column_span), jnp.float32)
    local_block = 0
    diagonal_block = ctx_rank * blocks_here + local_block
    listed = lax.dynamic_index_in_dim(attended_blocks, diagonal_block, 0, keepdims=False)
    query_portion = heads_of(query_proj)
    grad_heads = heads_of(grad_attn)
    attn_heads = heads_of(attn_parts)
    delta = jnp.einsum("ikgd,ikgd->kgi", grad_heads, attn_heads, preferred_element_type=jnp.float32)
    log_total = log_totals[local_block]

    def reverse_visit(slot_num, running):
        key_block_index = listed[slot_num]

        def reverse_live(present_block):
            query_gradient_total, key_buffer, value_buffer = present_block
            key_row_slice = load_key_block(all_keys, key_block_index, kv_heads)
            value_row_slice = load_key_block(all_values, key_block_index, kv_heads)
            score_matrix = causal_scores(
                query_portion, key_row_slice, key_block_index, diagonal_block
            )
            probs = jnp.exp(score_matrix - log_total[..., None])
            grad_probs = jnp.einsum(
                "ikgd,jkd->kgij", grad_heads, value_row_slice, preferred_element_type=jnp.float32
            )
            grad_scores = (score_scale * probs * (grad_probs - delta[..., None])).astype(
                jnp.bfloat16
            )
            query_gradient_total = query_gradient_total + jnp.einsum(
                "mayf,fmb->mayb", grad_scores, key_row_slice, preferred_element_type=jnp.float32
            )
            key_add = jnp.einsum(
                "kgij,ikgd->jkd", grad_scores, query_portion, preferred_element_type=jnp.float32
            ).reshape(BLOCK_TOKENS, -1)
            value_add = jnp.einsum(
                "kgij,ikgd->jkd",
                probs.astype(jnp.bfloat16),
                grad_heads,
                preferred_element_type=jnp.float32,
            ).reshape(BLOCK_TOKENS, -1)
            begin = key_block_index * BLOCK_TOKENS
            key_buffer = lax.dynamic_update_slice_in_dim(
                key_buffer,
                lax.dynamic_slice_in_dim(key_buffer, begin, BLOCK_TOKENS, 0) + key_add,
                begin,
                0,
            )
            value_buffer = lax.dynamic_update_slice_in_dim(
                value_buffer,
                lax.dynamic_slice_in_dim(value_buffer, begin, BLOCK_TOKENS, 0) + value_add,
                begin,
                0,
            )
            return (query_gradient_total, key_buffer, value_buffer)

        return lax.cond(
            key_block_index >= 0, reverse_live, lambda present_block: present_block, running
        )

    initial_state = (
        jnp.zeros((kv_heads, heads_per_group, BLOCK_TOKENS, HEAD_SIZE), jnp.float32),
        key_gradient_totals,
        value_gradient_totals,
    )
    query_gradient_total, key_gradient_totals, value_gradient_totals = lax.fori_loop(
        0, slot_count, reverse_visit, initial_state
    )
    query_grads = query_gradient_total.transpose(2, 0, 1, 3).reshape(BLOCK_TOKENS, head_cols)

    def to_window(buffer):
        padded = jnp.concatenate([jnp.zeros((front_rows, key_column_span), jnp.float32), buffer], 0)
        window_part = lax.dynamic_slice_in_dim(
            padded, front_rows - margin_rows + ctx_rank * local_rows, window_rows, 0
        )
        if use_far:
            far_part = lax.dynamic_slice_in_dim(
                padded, front_rows + (ctx_rank - far_step) * local_rows, local_rows, 0
            )
            return jnp.concatenate([window_part, far_part], 0)
        return window_part

    low_keys = to_window(key_gradient_totals).astype(jnp.bfloat16)
    low_values = to_window(value_gradient_totals).astype(jnp.bfloat16)
    grad_key = low_keys[margin_rows:window_rows].astype(jnp.float32)
    grad_value = low_values[margin_rows:window_rows].astype(jnp.float32)
    for distance in range(1, reach + 1):
        begin = (reach - distance) * local_rows
        back_keys, back_values = shifted(
            (low_keys[begin : begin + local_rows], low_values[begin : begin + local_rows]),
            "ctx",
            -distance,
        )
        grad_key = grad_key + back_keys.astype(jnp.float32)
        grad_value = grad_value + back_values.astype(jnp.float32)
    if use_far:
        far_back_keys, far_back_values = shifted(
            (low_keys[window_rows:], low_values[window_rows:]), "ctx", -far_step
        )
        grad_key = grad_key + far_back_keys.astype(jnp.float32)
        grad_value = grad_value + far_back_values.astype(jnp.float32)
    return (layer_out, query_grads, grad_key, grad_value, grad_wout)


def solution(mesh):
    return jax.shard_map(
        per_device,
        mesh=mesh,
        in_specs=(
            P("ctx", "head"),
            P("ctx", "head"),
            P("ctx", "head"),
            P("head", None),
            P(),
            P("ctx", "head"),
        ),
        out_specs=(
            P("ctx", "head"),
            P("ctx", "head"),
            P("ctx", "head"),
            P("ctx", "head"),
            P("head", "ctx"),
        ),
        check_vma=False,
    )
```

profile of v0, /device:TPU:0, one launch (start us, length us, event | category | flops | bytes accessed | tf_op | source)
XLA Modules:
  0.0 344.2 jit_solution(17926339508320888409)
XLA Ops:
  7.2 1.8 copy.33
  9.1 1.8 copy.35
  13.3 28.1 %all-gather.4.cloned.1.call-done = bf16[4096,256]{0,1:T(8,128)(2,1)} async-done(((bf16[512,256]{0,1:T(8,128)(2,1)}), bf16[4096,256]{0,1:T(8,128)(2,1)}) %all-gather.4.cloned.1.call-update) | async-done | bytes 2097168 | tf_op jit(solution)/shard_map/all_gather | solution.py:49
  41.4 30.7 %all-gather.6.cloned.1.call-done = bf16[4096,256]{0,1:T(8,128)(2,1)} async-done(((bf16[512,256]{0,1:T(8,128)(2,1)}), bf16[4096,256]{0,1:T(8,128)(2,1)}) %all-gather.6.cloned.1.call-update) | async-done | bytes 2097168 | tf_op jit(solution)/shard_map/all_gather | solution.py:50
  72.2 16.4 %while.34 = (s32[]{:T(128)}, f32[2,2,512]{2,1,0:T(2,128)S(1)}, f32[2,2,512]{2,1,0:T(2,128)S(1)}, f32[2,2,512,128]{3,2,1,0:T(8,128)S(1)}, s32[8]{0:T(128)S(1)}, /...) while((s32[]{:T(128)}, f32[2,2,512]{2,1,0:T(2,128)S(1)}, ...), condition=%wide.region_5.6_spmd, body=%wide.region_0.5_spmd.sunk | while | flops 549457920 | bytes 17957188 | solution.py:95
  73.4 6.2 %conditional.4 = ((f32[2,2,512]{2,1,0:T(2,128)S(1)}, f32[2,2,512]{2,1,0:T(2,128)S(1)}, f32[2,2,512,128]{3,2,1,0:T(8,128)S(1)})) conditional(s32[]{:T(128)} %convert_element_type.147, (f32[2,2,512]{2,1,0:T(2,128)S(1)}, f32[2,2,512]{2,1,0:T(2,128)S(1)}, f32[2,2,512,128]{3,2,1,0:T(8,128)S(1)}) %tuple.92, (s32[]{:T(128)}, s32[]{:T(128)}, ...), branch_computations={%region_1.1_spmd, %region_2.4_spmd} | conditional | flops 549457920 | bytes 17956956 | solution.py:86
  88.9 65.5 %all-gather.8.cloned.1.call-done = bf16[512,4096]{1,0:T(8,128)(2,1)} async-done(((bf16[512,1024]{1,0:T(8,128)(2,1)}), bf16[512,4096]{1,0:T(8,128)(2,1)}) %all-gather.8.cloned.1.call-update) | async-done | bytes 4194320 | tf_op jit(solution)/shard_map/all_gather | solution.py:105
  154.5 6.0 %fusion.28 = (f32[2,2,512]{2,1,0:T(2,128)S(1)}, bf16[2,2,512,128]{2,3,1,0:T(8,128)(2,1)S(1)}, bf16[512,512]{0,1:T(8,128)(2,1)S(1)}) fusion(f32[2,2,512,128]{2,3,1,0:T(8,128)S(1)} %copy.37, f32[2,2,512]{2,1,0:T(2,128)S(1)} %get-tuple-element.450, bf16[512,4096]{1,0:T(8,128)(2,1)} %all-gather.8.cloned.1.call-done, bf16[512,4096]{1,0:T(8,128)(2,1)} %param.17), kind=kOutput, calls=%fused_computation.47 | convolution fusion | flops 2149316608 | bytes 10502144 | tf_op jit(solution)/shard_map/dot_general | solution.py:106
  160.4 4.4 %convolution_convert_fusion = bf16[512,4096]{1,0:T(8,128)(2,1)} fusion(bf16[512,512]{0,1:T(8,128)(2,1)S(1)} %bitcast.108, bf16[512,4096]{1,0:T(8,128)(2,1)S(1)} %copy-done.4), kind=kOutput, calls=%fused_computation.41 | convolution fusion | flops 2149580800 | bytes 8912896 | tf_op jit(solution)/shard_map/dot_general | solution.py:109
  165.1 6.5 %convolution_convert_fusion.1 = bf16[512,4096]{1,0:T(8,128)(2,1)} fusion(bf16[512,512]{0,1:T(8,128)(2,1)S(1)} %bitcast.109, bf16[512,4096]{1,0:T(8,128)(2,1)} %param.17), kind=kOutput, calls=%fused_computation.42 | convolution fusion | flops 2149580800 | bytes 8912896 | tf_op jit(solution)/shard_map/dot_general | solution.py:101
  171.7 2.4 broadcast.29.clone
  174.2 2.5 broadcast.29
  176.6 21.7 %while.35 = (s32[]{:T(128)}, f32[2,2,512,128]{3,2,1,0:T(8,128)S(1)}, f32[4096,256]{0,1:T(8,128)}, f32[4096,256]{0,1:T(8,128)}, s32[8]{0:T(128)S(1)}, /*index=5*/...) while((s32[]{:T(128)}, ...), condition=%wide.region_10.11_spmd, body=%wide.region_7.0_spmd.sunk | while | flops 1354760192 | bytes 29909372 | solution.py:182
  177.9 11.6 %conditional.5 = ((f32[2,2,512,128]{3,2,1,0:T(8,128)S(1)}, f32[4096,256]{0,1:T(8,128)}, f32[4096,256]{0,1:T(8,128)})) conditional(s32[]{:T(128)} %convert_element_type.148, (f32[2,2,512,128]{3,2,1,0:T(8,128)S(1)}, f32[4096,256]{0,1:T(8,128)}, f32[4096,256]{0,1:T(8,128)}) %tuple.95, (s32[]{:T(128)}, s32[]{:T(128)}, bf16[4096,256]{0,1:T(8,128)(2,1)}, ...), branch_computations={%region_8.8_spmd, %region_9.9_spmd} | conditional | flops 1354760192 | bytes 29909092 | solution.py:173
  187.1 2.4 constant_dynamic-update-slice_fusion
  198.4 4.6 %copy.40 = bf16[4096,256]{1,0:T(8,128)(2,1)} copy(f32[4096,256]{0,1:T(8,128)} %get-tuple-element.454) | data formatting | bytes 6291456 | tf_op jit(solution)/shard_map/while | solution.py:182
  213.3 4.7 %copy.39 = bf16[4096,256]{1,0:T(8,128)(2,1)} copy(f32[4096,256]{0,1:T(8,128)} %get-tuple-element.453) | data formatting | bytes 6291456 | tf_op jit(solution)/shard_map/while | solution.py:182
  223.1 74.6 %collective-permute-done.13 = bf16[512,256]{1,0:T(8,128)(2,1)} collective-permute-done((bf16[512,256]{1,0:T(8,128)(2,1)S(1)}, bf16[512,256]{1,0:T(8,128)(2,1)}, u32[]{:S(2)}, u32[]{:S(2)}) %collective-permute-start.13) | collective-permute-done | bytes 262176 | tf_op jit(solution)/shard_map/ppermute | solution.py:13
  302.7 1.8 reshape.49
  309.7 15.4 %collective-permute-done.6 = bf16[512,256]{1,0:T(8,128)(2,1)} collective-permute-done((bf16[512,256]{1,0:T(8,128)(2,1)}, bf16[512,256]{1,0:T(8,128)(2,1)}, u32[]{:S(2)}, u32[]{:S(2)}) %collective-permute-start.6) | collective-permute-done | bytes 262176 | tf_op jit(solution)/shard_map/ppermute | solution.py:13
  326.4 2.6 convert_add_fusion
  329.0 3.8 %collective-permute-done.3 = bf16[512,256]{1,0:T(8,128)(2,1)S(1)} collective-permute-done((bf16[512,256]{1,0:T(8,128)(2,1)S(1)}, bf16[512,256]{1,0:T(8,128)(2,1)S(1)}, u32[]{:S(2)}, u32[]{:S(2)}) %collective-permute-start.3) | collective-permute-done | bytes 262176 | tf_op jit(solution)/shard_map/ppermute | solution.py:13
  333.4 2.2 convert_add_fusion.1
  335.5 2.1 convert_element_type.114
  (107 shorter events, 52.7 us)
Async XLA Ops:
  7.2 6.1 %copy-start = (s32[8,8]{1,0:T(8,128)S(1)}, s32[8,8]{1,0:T(8,128)}, u32[]{:S(2)}) copy-start(s32[8,8]{1,0:T(8,128)} %param.18) | copy-start | bytes 772
  7.2 34.2 %all-gather.4.cloned.1.call-start = ((), (), s32[]{:S(2)}) async-start(), calls=%async_computation.2 | async-start | bytes 2359296 | tf_op jit(solution)/shard_map/all_gather | solution.py:49
  9.0 63.0 %all-gather.6.cloned.1.call-start = ((), (), s32[]{:S(2)}) async-start(), calls=%async_computation.3 | async-start | bytes 2359296 | tf_op jit(solution)/shard_map/all_gather | solution.py:50
  10.9 143.5 %all-gather.8.cloned.1.call-start = ((), (), s32[]{:S(2)}) async-start(), calls=%async_computation.5 | async-start | bytes 5242880 | tf_op jit(solution)/shard_map/all_gather | solution.py:105
  11.7 323.9 %reduce-scatter.5.cloned.1.call-start = ((), (), s32[]{:S(2)}) async-start(), calls=%async_computation.6 | async-start | bytes 4718592 | tf_op jit(solution)/shard_map/reduce_scatter | solution.py:115
  154.4 6.0 %copy-start.4 = (bf16[512,4096]{1,0:T(8,128)(2,1)S(1)}, bf16[512,4096]{1,0:T(8,128)(2,1)}, u32[]{:S(2)}) copy-start(bf16[512,4096]{1,0:T(8,128)(2,1)} %all-gather.8.cloned.1.call-done) | copy-start | bytes 12582916
  164.8 172.8 %reduce-scatter.3.cloned.1.call-start = ((), (), s32[]{:S(2)}) async-start(), calls=%async_computation.4 | async-start | bytes 5242880 | tf_op jit(solution)/shard_map/reduce_scatter | solution.py:102
  204.6 1.3 copy-start.2
  206.8 15.0 %collective-permute-start.7 = (bf16[512,256]{1,0:T(8,128)(2,1)S(1)}, bf16[512,256]{1,0:T(8,128)(2,1)}, u32[]{:S(2)}, u32[]{:S(2)}) collective-permute-start(bf16[512,256]{1,0:T(8,128)(2,1)S(1)} %get-tuple-element.525), channel_id=1, source_target_pairs={{4,0},{8,4},{12,8},{16,12},{20,16},{24,20},{28,24},{5,1},{9,5},{13... | collective-permute-start | bytes 786440 | tf_op jit(solution)/shard_map/ppermute | solution.py:13
  208.1 89.6 %collective-permute-start.13 = (bf16[512,256]{1,0:T(8,128)(2,1)S(1)}, bf16[512,256]{1,0:T(8,128)(2,1)}, u32[]{:S(2)}, u32[]{:S(2)}) collective-permute-start(bf16[512,256]{1,0:T(8,128)(2,1)S(1)} %get-tuple-element.526), channel_id=1, source_target_pairs={{28,0},{29,1},{30,2},{31,3}} | collective-permute-start | bytes 786440 | tf_op jit(solution)/shard_map/ppermute | solution.py:13
  209.4 89.6 %collective-permute-start.12 = (bf16[512,256]{1,0:T(8,128)(2,1)S(1)}, bf16[512,256]{1,0:T(8,128)(2,1)}, u32[]{:S(2)}, u32[]{:S(2)}) collective-permute-start(bf16[512,256]{1,0:T(8,128)(2,1)S(1)} %get-tuple-element.527), channel_id=1, source_target_pairs={{24,0},{28,4},{25,1},{29,5},{26,2},{30,6},{27,3},{31,7}} | collective-permute-start | bytes 786440 | tf_op jit(solution)/shard_map/ppermute | solution.py:13
  210.7 89.6 %collective-permute-start.11 = (bf16[512,256]{1,0:T(8,128)(2,1)S(1)}, bf16[512,256]{1,0:T(8,128)(2,1)}, u32[]{:S(2)}, u32[]{:S(2)}) collective-permute-start(bf16[512,256]{1,0:T(8,128)(2,1)S(1)} %get-tuple-element.528), channel_id=1, source_target_pairs={{20,0},{24,4},{28,8},{21,1},{25,5},{29,9},{22,2},{26,6},{30,10},{2... | collective-permute-start | bytes 786440 | tf_op jit(solution)/shard_map/ppermute | solution.py:13
  212.0 92.5 %collective-permute-start.10 = (bf16[512,256]{1,0:T(8,128)(2,1)}, bf16[512,256]{1,0:T(8,128)(2,1)}, u32[]{:S(2)}, u32[]{:S(2)}) collective-permute-start(bf16[512,256]{1,0:T(8,128)(2,1)} %get-tuple-element.529), channel_id=1, source_target_pairs={{16,0},{20,4},{24,8},{28,12},{17,1},{21,5},{25,9},{29,13},{18,2},{... | collective-permute-start | bytes 786440 | tf_op jit(solution)/shard_map/ppermute | solution.py:13
  219.5 1.4 copy-start.3
  221.8 84.0 %collective-permute-start.9 = (bf16[512,256]{1,0:T(8,128)(2,1)}, bf16[512,256]{1,0:T(8,128)(2,1)}, u32[]{:S(2)}, u32[]{:S(2)}) collective-permute-start(bf16[512,256]{1,0:T(8,128)(2,1)} %get-tuple-element.530), channel_id=1, source_target_pairs={{12,0},{16,4},{20,8},{24,12},{28,16},{13,1},{17,5},{21,9},{25,13},... | collective-permute-start | bytes 786440 | tf_op jit(solution)/shard_map/ppermute | solution.py:13
  297.7 9.4 %collective-permute-start.8 = (bf16[512,256]{1,0:T(8,128)(2,1)}, bf16[512,256]{1,0:T(8,128)(2,1)}, u32[]{:S(2)}, u32[]{:S(2)}) collective-permute-start(bf16[512,256]{1,0:T(8,128)(2,1)} %get-tuple-element.531), channel_id=1, source_target_pairs={{8,0},{12,4},{16,8},{20,12},{24,16},{28,20},{9,1},{13,5},{17,9},{2... | collective-permute-start | bytes 786440 | tf_op jit(solution)/shard_map/ppermute | solution.py:13
  299.0 9.4 %collective-permute-start = (bf16[512,256]{1,0:T(8,128)(2,1)}, bf16[512,256]{1,0:T(8,128)(2,1)}, u32[]{:S(2)}, u32[]{:S(2)}) collective-permute-start(bf16[512,256]{1,0:T(8,128)(2,1)} %get-tuple-element.532), channel_id=1, source_target_pairs={{4,0},{8,4},{12,8},{16,12},{20,16},{24,20},{28,24},{5,1},{9,5},{13... | collective-permute-start | bytes 786440 | tf_op jit(solution)/shard_map/ppermute | solution.py:13
  300.3 24.8 %collective-permute-start.6 = (bf16[512,256]{1,0:T(8,128)(2,1)}, bf16[512,256]{1,0:T(8,128)(2,1)}, u32[]{:S(2)}, u32[]{:S(2)}) collective-permute-start(bf16[512,256]{1,0:T(8,128)(2,1)} %get-tuple-element.533), channel_id=1, source_target_pairs={{28,0},{29,1},{30,2},{31,3}} | collective-permute-start | bytes 786440 | tf_op jit(solution)/shard_map/ppermute | solution.py:13
  301.8 35.8 %copy-start.1 = (s32[8,8]{1,0:T(8,128)S(1)}, s32[8,8]{1,0:T(8,128)}, u32[]{:S(2)}) copy-start(s32[8,8]{1,0:T(8,128)} %param.18) | copy-start | bytes 772
  304.5 24.5 %collective-permute-start.5 = (bf16[512,256]{1,0:T(8,128)(2,1)S(1)}, bf16[512,256]{1,0:T(8,128)(2,1)S(1)}, u32[]{:S(2)}, u32[]{:S(2)}) collective-permute-start(bf16[512,256]{1,0:T(8,128)(2,1)S(1)} %get-tuple-element.534), channel_id=1, source_target_pairs={{24,0},{28,4},{25,1},{29,5},{26,2},{30,6},{27,3},{31,7}} | collective-permute-start | bytes 786440 | tf_op jit(solution)/shard_map/ppermute | solution.py:13
  305.8 23.2 %collective-permute-start.4 = (bf16[512,256]{1,0:T(8,128)(2,1)S(1)}, bf16[512,256]{1,0:T(8,128)(2,1)S(1)}, u32[]{:S(2)}, u32[]{:S(2)}) collective-permute-start(bf16[512,256]{1,0:T(8,128)(2,1)S(1)} %get-tuple-element.535), channel_id=1, source_target_pairs={{20,0},{24,4},{28,8},{21,1},{25,5},{29,9},{22,2},{26,6},{30,10},{2... | collective-permute-start | bytes 786440 | tf_op jit(solution)/shard_map/ppermute | solution.py:13
  307.1 25.7 %collective-permute-start.3 = (bf16[512,256]{1,0:T(8,128)(2,1)S(1)}, bf16[512,256]{1,0:T(8,128)(2,1)S(1)}, u32[]{:S(2)}, u32[]{:S(2)}) collective-permute-start(bf16[512,256]{1,0:T(8,128)(2,1)S(1)} %get-tuple-element.536), channel_id=1, source_target_pairs={{16,0},{20,4},{24,8},{28,12},{17,1},{21,5},{25,9},{29,13},{18,2},{... | collective-permute-start | bytes 786440 | tf_op jit(solution)/shard_map/ppermute | solution.py:13
  308.4 24.4 %collective-permute-start.2 = (bf16[512,256]{1,0:T(8,128)(2,1)S(1)}, bf16[512,256]{1,0:T(8,128)(2,1)S(1)}, u32[]{:S(2)}, u32[]{:S(2)}) collective-permute-start(bf16[512,256]{1,0:T(8,128)(2,1)S(1)} %get-tuple-element.537), channel_id=1, source_target_pairs={{12,0},{16,4},{20,8},{24,12},{28,16},{13,1},{17,5},{21,9},{25,13},... | collective-permute-start | bytes 786440 | tf_op jit(solution)/shard_map/ppermute | solution.py:13
  325.1 8.3 %collective-permute-start.1 = (bf16[512,256]{1,0:T(8,128)(2,1)S(1)}, bf16[512,256]{1,0:T(8,128)(2,1)S(1)}, u32[]{:S(2)}, u32[]{:S(2)}) collective-permute-start(bf16[512,256]{1,0:T(8,128)(2,1)S(1)} %get-tuple-element.538), channel_id=1, source_target_pairs={{8,0},{12,4},{16,8},{20,12},{24,16},{28,20},{9,1},{13,5},{17,9},{2... | collective-permute-start | bytes 786440 | tf_op jit(solution)/shard_map/ppermute | solution.py:13
Sparse Core Ops, SparseCore 0:
  10.5 30.8 all-gather.3
  43.8 28.1 all-gather.5
  73.7 80.7 all-gather.7
  165.0 49.8 reduce-scatter.4
  217.7 76.7 reduce-scatter.2
where the time goes:
time: 348 us; the launch traced here: 344 us
  waiting for transfers between devices  220 us (63%)
  local copies, waits for them, and re-layouts  42.4 us (12%)
  matrix products  25.5 us (7%)
  starting transfers between devices  18.6 us (5%)
  between operations  14.1 us (4%)
  loops' own time  13.7 us (4%)
  other arithmetic  10.3 us (3%)
    ppermute x14, waiting for transfers between devices, shifted(): lax.ppermute(value, axis, [(source, source + steps) for source in range(l...  94.5 us
    all_gather x1, waiting for transfers between devices, per_device(): piece = lax.all_gather(grad_out, 'head', axis=1, tiled=True)  65.5 us
    all_gather x1, waiting for transfers between devices, per_device(): lax.all_gather(projected_values, 'ctx', axis=0, tiled=True)  30.7 us
    all_gather x1, waiting for transfers between devices, per_device(): lax.all_gather(projected_keys, 'ctx', axis=0, tiled=True)  28.1 us
    ppermute x14, starting transfers between devices, shifted(): lax.ppermute(value, axis, [(source, source + steps) for source in range(l...  18.3 us
    while x2, local copies, waits for them, and re-layouts, per_device(): lax.fori_loop(0, slot_count, reverse_visit, initial_state)  9.29 us
    unnamed x13, local copies, waits for them, and re-layouts  7.54 us
  transfers between devices with their start and end apart: 19, of which 7 were waited for; matrix products, arithmetic and copies ran while one was open for 18% of the time, Pallas kernels for 0%

commit v1 on v0

--- a/solution.py
+++ b/solution.py
@@ -1,6 +1,11 @@
+import functools
+import math
+
 import jax
 import jax.numpy as jnp
 from jax import lax
+from jax.experimental import pallas as pl
+from jax.experimental.pallas import tpu as pltpu
 from jax.sharding import PartitionSpec as P
 
 HEAD_SIZE = 128
@@ -28,7 +33,7 @@
     return jnp.where(allowed, raw_scores, -jnp.inf)
 
 
-def per_device(query_proj, projected_keys, projected_values, w_out, attended_blocks, grad_out):
+def general_device(query_proj, projected_keys, projected_values, w_out, attended_blocks, grad_out):
     ctx_rank = lax.axis_index("ctx")
     ctx_count = lax.axis_size("ctx")
     local_rows = query_proj.shape[0]
@@ -218,6 +223,401 @@
     return (layer_out, query_grads, grad_key, grad_value, grad_wout)
 
 
+MESH = pl.DeviceIdType.MESH
+VMEM_BYTES = 48 * 1024 * 1024
+EXP2_SCALE = HEAD_SIZE ** (-0.5) * math.log2(math.e)
+CONTRACT_LAST = (((1,), (1,)), ((), ()))
+CONTRACT_FIRST = (((0,), (0,)), ((), ()))
+
+
+def dot(left, right, dims=(((1,), (0,)), ((), ()))):
+    return lax.dot_general(left, right, dims, preferred_element_type=jnp.float32)
+
+
+def greet(peers, count):
+    barrier = pltpu.get_barrier_semaphore()
+    for peer in peers:
+        pl.semaphore_signal(barrier, inc=1, device_id={"ctx": peer}, device_id_type=MESH)
+    pl.semaphore_wait(barrier, count)
+
+
+def remote(source, target, send_sem, recv_sem, peer):
+    return pltpu.make_async_remote_copy(
+        src_ref=source,
+        dst_ref=target,
+        send_sem=send_sem,
+        recv_sem=recv_sem,
+        device_id={"ctx": peer},
+        device_id_type=MESH,
+    )
+
+
+def spread_kernel(count, kv_ref, q_ref, kv_all, q_units, send, recv, q_send, q_recv, local):
+    me = lax.axis_index("ctx")
+    core = lax.rem(me, 2)
+    sibling = me + 1 - 2 * core
+    across = count - 2 - (me - core)
+    greet([lax.rem(me + step, count) for step in range(1, count)], count - 1)
+    copies = []
+    for step in range(1, count):
+        peer = lax.rem(me + step, count)
+        copy = remote(
+            kv_ref.at[lax.rem(peer, 2)], kv_all.at[me], send.at[step], recv.at[step], peer
+        )
+        copy.start()
+        copies.append(copy)
+
+    @pl.when(core == 0)
+    def _():
+        remote(q_ref.at[1], q_units.at[0], q_send.at[0], q_recv.at[0], sibling).start()
+        mine = pltpu.make_async_copy(q_ref.at[0], q_units.at[0], local.at[1])
+        mine.start()
+        mine.wait()
+
+    @pl.when(core == 1)
+    def _():
+        remote(q_ref.at[0], q_units.at[1], q_send.at[0], q_recv.at[1], across).start()
+        remote(q_ref.at[1], q_units.at[1], q_send.at[1], q_recv.at[1], across + 1).start()
+
+    mine = pltpu.make_async_copy(kv_ref.at[core], kv_all.at[me], local.at[0])
+    mine.start()
+    mine.wait()
+    for copy in copies:
+        copy.wait()
+
+    remote(q_ref.at[0], q_units.at[1], q_send.at[0], q_recv.at[1], across).wait()
+
+    @pl.when(core == 1)
+    def _():
+        remote(q_ref.at[1], q_units.at[0], q_send.at[1], q_recv.at[0], sibling).wait()
+
+
+def return_kernel(count, dkv_ref, dq_ref, dkv_all, dq_halves, send, recv, q_send, q_recv, local):
+    me = lax.axis_index("ctx")
+    core = lax.rem(me, 2)
+    sibling = me + 1 - 2 * core
+    across = count - 2 - (me - core)
+    greet([lax.rem(me + step, count) for step in range(1, count)], count - 1)
+    copies = []
+    for step in range(1, count):
+        peer = lax.rem(me + step, count)
+        copy = remote(dkv_ref.at[peer], dkv_all.at[me], send.at[step], recv.at[step], peer)
+        copy.start()
+        copies.append(copy)
+    remote(dq_ref.at[1], dq_halves.at[core], q_send.at[0], q_recv.at[core], across + 1).start()
+
+    @pl.when(core == 1)
+    def _():
+        remote(dq_ref.at[0], dq_halves.at[1], q_send.at[1], q_recv.at[1], sibling).start()
+
+    @pl.when(core == 0)
+    def _():
+        mine = pltpu.make_async_copy(dq_ref.at[0], dq_halves.at[0], local.at[1])
+        mine.start()
+        mine.wait()
+
+    mine = pltpu.make_async_copy(dkv_ref.at[me], dkv_all.at[me], local.at[0])
+    mine.start()
+    mine.wait()
+    for copy in copies:
+        copy.wait()
+    remote(dq_ref.at[1], dq_halves.at[1], q_send.at[0], q_recv.at[1], across + 1).wait()
+
+    @pl.when(core == 1)
+    def _():
+        remote(dq_ref.at[0], dq_halves.at[0], q_send.at[1], q_recv.at[0], across).wait()
+
+
+def exchange(body, collective_id, count, blocks, units):
+    any_space = pl.BlockSpec(memory_space=pl.ANY)
+    return pl.pallas_call(
+        functools.partial(body, count),
+        out_shape=(
+            jax.ShapeDtypeStruct((count,) + blocks.shape[1:], blocks.dtype),
+            jax.ShapeDtypeStruct(units.shape, units.dtype),
+        ),
+        in_specs=[any_space, any_space],
+        out_specs=(any_space, any_space),
+        scratch_shapes=[
+            pltpu.SemaphoreType.DMA((count,)),
+            pltpu.SemaphoreType.DMA((count,)),
+            pltpu.SemaphoreType.DMA((2,)),
+            pltpu.SemaphoreType.DMA((2,)),
+            pltpu.SemaphoreType.DMA((2,)),
+        ],
+        compiler_params=pltpu.CompilerParams(
+            collective_id=collective_id, has_side_effects=True, vmem_limit_bytes=VMEM_BYTES
+        ),
+        cost_estimate=pl.CostEstimate(
+            flops=0, bytes_accessed=2 * blocks.size * 2 + units.size * 4, transcendentals=0
+        ),
+    )(blocks, units)
+
+
+def head_part(value, head):
+    return value[:, head * HEAD_SIZE : (head + 1) * HEAD_SIZE]
+
+
+def diagonal_mask(scores):
+    key_row = lax.broadcasted_iota(jnp.int32, scores.shape, 0)
+    query_col = lax.broadcasted_iota(jnp.int32, scores.shape, 1)
+    return jnp.where(key_row <= query_col, scores, -jnp.inf)
+
+
+def forward_kernel(rows_ref, q_ref, kv_ref, attn_ref, total_ref, largest, denominator, weighted):
+    unit = pl.program_id(0)
+    heads = q_ref.shape[2] // HEAD_SIZE
+
+    def visit(block, diagonal):
+        keys = kv_ref[block, :, :HEAD_SIZE]
+        values = kv_ref[block, :, HEAD_SIZE:]
+        for head in range(heads):
+            at = pl.ds(head, 1)
+            scores = dot(keys, head_part(q_ref[0], head), CONTRACT_LAST)
+            if diagonal:
+                scores = diagonal_mask(scores)
+            top = jnp.max(scores, 0, keepdims=True)
+            if not diagonal:
+                before = largest[at, :]
+                top = jnp.maximum(before, top)
+                rescale = jnp.exp2((before - top) * EXP2_SCALE)
+            weights = jnp.exp2(scores * EXP2_SCALE - top * EXP2_SCALE)
+            added = jnp.sum(weights, 0, keepdims=True)
+            product = dot(values, weights.astype(jnp.bfloat16), CONTRACT_FIRST)
+            largest[at, :] = top
+            if diagonal:
+                denominator[at, :] = added
+                weighted[head] = product
+            else:
+                denominator[at, :] = denominator[at, :] * rescale + added
+                weighted[head] = weighted[head] * rescale + product
+
+    visit(rows_ref[unit, 0], True)
+
+    @pl.loop(1, rows_ref.shape[1])
+    def _(slot):
+        block = rows_ref[unit, slot]
+
+        @pl.when(block >= 0)
+        def _():
+            visit(block, False)
+
+    for head in range(heads):
+        at = pl.ds(head, 1)
+        bottom = denominator[at, :]
+        attn_ref[0, :, head * HEAD_SIZE : (head + 1) * HEAD_SIZE] = (
+            (weighted[head] / bottom).T.astype(jnp.bfloat16)
+        )
+        total_ref[0, at, :] = largest[at, :] * EXP2_SCALE + jnp.log2(bottom)
+
+
+def forward_units(rows, q_units, kv_all):
+    units, tokens, width = q_units.shape
+    heads = width // HEAD_SIZE
+    whole = pl.BlockSpec(kv_all.shape, lambda unit, rows: (0, 0, 0))
+    per_unit = pl.BlockSpec((1, tokens, width), lambda unit, rows: (unit, 0, 0))
+    per_total = pl.BlockSpec((1, heads, tokens), lambda unit, rows: (unit, 0, 0))
+    return pl.pallas_call(
+        forward_kernel,
+        grid_spec=pltpu.PrefetchScalarGridSpec(
+            num_scalar_prefetch=1,
+            grid=(units,),
+            in_specs=[per_unit, whole],
+            out_specs=(per_unit, per_total),
+            scratch_shapes=[
+                pltpu.VMEM((heads, tokens), jnp.float32),
+                pltpu.VMEM((heads, tokens), jnp.float32),
+                pltpu.VMEM((heads, HEAD_SIZE, tokens), jnp.float32),
+            ],
+        ),
+        out_shape=(
+            jax.ShapeDtypeStruct(q_units.shape, jnp.bfloat16),
+            jax.ShapeDtypeStruct((units, heads, tokens), jnp.float32),
+        ),
+        compiler_params=pltpu.CompilerParams(vmem_limit_bytes=VMEM_BYTES),
+        cost_estimate=pl.CostEstimate(
+            flops=20 * tokens * tokens * width,
+            bytes_accessed=kv_all.size * 2,
+            transcendentals=5 * tokens * tokens * heads,
+        ),
+    )(rows, q_units, kv_all)
+
+
+def backward_kernel(
+    rows_ref, q_ref, g_ref, attn_ref, total_ref, kv_ref, dq_ref, dkv_ref, delta, dq_sum, dkv_sum
+):
+    unit = pl.program_id(0)
+    heads = q_ref.shape[2] // HEAD_SIZE
+    score_scale = HEAD_SIZE ** (-0.5)
+
+    @pl.when(unit == 0)
+    def _():
+        dkv_sum[...] = jnp.zeros_like(dkv_sum)
+
+    for head in range(heads):
+        product = head_part(g_ref[0], head).astype(jnp.float32) * head_part(
+            attn_ref[0], head
+        ).astype(jnp.float32)
+        delta[pl.ds(head, 1), :] = jnp.sum(product.T, 0, keepdims=True)
+
+    def visit(block, diagonal):
+        keys = kv_ref[block, :, :HEAD_SIZE]
+        values = kv_ref[block, :, HEAD_SIZE:]
+        key_sum, value_sum = None, None
+        for head in range(heads):
+            at = pl.ds(head, 1)
+            queries = head_part(q_ref[0], head)
+            grads = head_part(g_ref[0], head)
+            scores = dot(keys, queries, CONTRACT_LAST)
+            if diagonal:
+                scores = diagonal_mask(scores)
+            probs = jnp.exp2(scores * EXP2_SCALE - total_ref[0, at, :])
+            grad_probs = dot(values, grads, CONTRACT_LAST)
+            grad_scores = (probs * (grad_probs - delta[at, :])).astype(jnp.bfloat16)
+            value_add = dot(probs.astype(jnp.bfloat16), grads)
+            key_add = dot(grad_scores, queries)
+            query_add = dot(keys, grad_scores, CONTRACT_FIRST)
+            dq_sum[head] = query_add if diagonal else dq_sum[head] + query_add
+            key_sum = key_add if head == 0 else key_sum + key_add
+            value_sum = value_add if head == 0 else value_sum + value_add
+        dkv_sum[block, :, :HEAD_SIZE] += key_sum * score_scale
+        dkv_sum[block, :, HEAD_SIZE:] += value_sum
+
+    visit(rows_ref[unit, 0], True)
+
+    @pl.loop(1, rows_ref.shape[1])
+    def _(slot):
+        block = rows_ref[unit, slot]
+
+        @pl.when(block >= 0)
+        def _():
+            visit(block, False)
+
+    for head in range(heads):
+        dq_ref[0, :, head * HEAD_SIZE : (head + 1) * HEAD_SIZE] = (
+            (dq_sum[head] * score_scale).T.astype(dq_ref.dtype)
+        )
+
+    @pl.when(unit == pl.num_programs(0) - 1)
+    def _():
+        dkv_ref[...] = dkv_sum[...].astype(dkv_ref.dtype)
+
+
+def backward_units(rows, q_units, g_units, attn_units, totals, kv_all):
+    units, tokens, width = q_units.shape
+    heads = width // HEAD_SIZE
+    whole = pl.BlockSpec(kv_all.shape, lambda unit, rows: (0, 0, 0))
+    per_unit = pl.BlockSpec((1, tokens, width), lambda unit, rows: (unit, 0, 0))
+    per_total = pl.BlockSpec((1, heads, tokens), lambda unit, rows: (unit, 0, 0))
+    return pl.pallas_call(
+        backward_kernel,
+        grid_spec=pltpu.PrefetchScalarGridSpec(
+            num_scalar_prefetch=1,
+            grid=(units,),
+            in_specs=[per_unit, per_unit, per_unit, per_total, whole],
+            out_specs=(per_unit, whole),
+            scratch_shapes=[
+                pltpu.VMEM((heads, tokens), jnp.float32),
+                pltpu.VMEM((heads, HEAD_SIZE, tokens), jnp.float32),
+                pltpu.VMEM(kv_all.shape, jnp.float32),
+            ],
+        ),
+        out_shape=(
+            jax.ShapeDtypeStruct(q_units.shape, jnp.bfloat16),
+            jax.ShapeDtypeStruct(kv_all.shape, jnp.bfloat16),
+        ),
+        compiler_params=pltpu.CompilerParams(vmem_limit_bytes=VMEM_BYTES),
+        cost_estimate=pl.CostEstimate(
+            flops=50 * tokens * tokens * width,
+            bytes_accessed=kv_all.size * 4,
+            transcendentals=5 * tokens * tokens * heads,
+        ),
+    )(rows, q_units, g_units, attn_units, totals, kv_all)
+
+
+def halves_of(value):
+    half = value.shape[1] // 2
+    return jnp.stack([value[:, :half], value[:, half:]])
+
+
+def to_units(home, core, count):
+    first, second = home[0], home[1]
+    even = range(0, count, 2)
+    one = lax.ppermute(
+        jnp.where(core == 0, second, first),
+        "ctx",
+        [(c, c + 1) for c in even] + [(c + 1, count - 2 - c) for c in even],
+    )
+    two = lax.ppermute(second, "ctx", [(c + 1, count - 1 - c) for c in even])
+    return jnp.stack([jnp.where(core == 0, first, one), jnp.where(core == 0, one, two)])
+
+
+def to_home(units, core, count):
+    even = range(0, count, 2)
+    one = lax.ppermute(
+        jnp.where(core == 0, units[1], units[0]),
+        "ctx",
+        [(c, count - 1 - c) for c in even] + [(c + 1, c) for c in even],
+    )
+    two = lax.ppermute(units[1], "ctx", [(c + 1, count - 1 - c) for c in even])
+    return jnp.concatenate(
+        [jnp.where(core == 0, units[0], one), jnp.where(core == 0, one, two)], 1
+    )
+
+
+def paired_device(query_proj, projected_keys, projected_values, w_out, attended_blocks, grad_out):
+    count = lax.axis_size("ctx")
+    me = lax.axis_index("ctx")
+    core = lax.rem(me, 2)
+    tokens = query_proj.shape[0]
+    piece = lax.all_gather(grad_out, "head", axis=1, tiled=True)
+    key_halves, value_halves = halves_of(projected_keys), halves_of(projected_values)
+    kv_all, q_units = exchange(
+        spread_kernel,
+        0,
+        count,
+        jnp.concatenate([key_halves, value_halves], 2),
+        halves_of(query_proj),
+    )
+    own_even = me - core
+    rows = jnp.take(attended_blocks, jnp.stack([own_even, count - 1 - own_even]), axis=0)
+    attn_units, totals = forward_units(rows, q_units, kv_all)
+    attn = to_home(attn_units, core, count)
+    out_terms = dot(attn, w_out)
+    layer_out = lax.psum_scatter(
+        out_terms.astype(jnp.bfloat16), "head", scatter_dimension=1, tiled=True
+    )
+    grad_attn = dot(piece, w_out, CONTRACT_LAST).astype(jnp.bfloat16)
+    g_units = to_units(halves_of(grad_attn), core, count)
+    weight_terms = dot(attn, piece, CONTRACT_FIRST)
+    grad_wout = lax.psum_scatter(
+        weight_terms.astype(jnp.bfloat16), "ctx", scatter_dimension=1, tiled=True
+    ).astype(jnp.float32)
+    dq_units, dkv = backward_units(rows, q_units, g_units, attn_units, totals, kv_all)
+    dkv_all, dq_halves = exchange(return_kernel, 1, count, dkv, dq_units)
+    grad_query = jnp.concatenate([dq_halves[0], dq_halves[1]], 1).astype(jnp.float32)
+    summed = jnp.sum(
+        dkv_all.reshape(count // 2, 2, tokens, 2 * HEAD_SIZE).astype(jnp.float32), 0
+    )
+    grad_key = jnp.concatenate([summed[0, :, :HEAD_SIZE], summed[1, :, :HEAD_SIZE]], 1)
+    grad_value = jnp.concatenate([summed[0, :, HEAD_SIZE:], summed[1, :, HEAD_SIZE:]], 1)
+    return (layer_out, grad_query, grad_key, grad_value, grad_wout)
+
+
+def per_device(query_proj, projected_keys, projected_values, w_out, attended_blocks, grad_out):
+    count = lax.axis_size("ctx")
+    pairs = (
+        projected_keys.shape[1] == 2 * HEAD_SIZE
+        and query_proj.shape[0] == BLOCK_TOKENS
+        and count % 4 == 0
+        and attended_blocks.shape[1] >= count
+    )
+    body = paired_device if pairs else general_device
+    return body(
+        query_proj, projected_keys, projected_values, w_out, attended_blocks, grad_out
+    )
+
+
 def solution(mesh):
     return jax.shard_map(
         per_device,

time: 348 us -> 251 us (0.72)
  waiting for transfers between devices: 220 us -> 104 us
  Pallas kernels: 0 us -> 101 us
  local copies, waits for them, and re-layouts: 42.4 us -> 3.77 us
  starting transfers between devices: 18.6 us -> 1.77 us
  loops' own time: 13.7 us -> 0 us
  matrix products: 25.5 us -> 19.8 us
  other arithmetic: 10.3 us -> 6.53 us
    pallas_call x0 -> x4, Pallas kernels: none -> 101 us  [the longest x2 71.6 us: exchange(): pl.pallas_call(functools.partial(body, count), out_shape=(jax.ShapeDtypeS...]
    all_gather x3 -> x1, waiting for transfers between devices: 124 us -> 33.7 us  [paired_device(): piece = lax.all_gather(grad_out, 'head', axis=1, tiled=True)]
    ppermute x14 -> x4, waiting for transfers between devices: 94.5 us -> 10 us  [the longest x1 6.68 us: to_units(): lax.ppermute(jnp.where(core == 0, second, first), 'ctx', [(c, c + 1) for...]
    reduce_scatter x2, waiting for transfers between devices: 0.01 us -> 59.6 us  [the longest x1 59.6 us: paired_device(): lax.psum_scatter(out_terms.astype(jnp.bfloat16), 'head', scatter_dimensio...]
    ppermute x14 -> x4, starting transfers between devices: 18.3 us -> 1.65 us  [the longest x1 0.86 us: to_units(): two = lax.ppermute(second, 'ctx', [(c + 1, count - 1 - c) for c in even])]
    another operation x18 -> x0, loops' own time: 13.7 us -> none  [the longest x1 5.44 us: per_device(): lax.fori_loop(0, slot_count, forward_visit, initial_state)]
    dynamic_slice x19 -> x0, local copies, waits for them, and re-layouts: 12.4 us -> none  [the longest x8 4.69 us: forward_visit(): key_block_index = listed[slot_num]]
    while x4 -> x0, local copies, waits for them, and re-layouts: 9.89 us -> none  [the longest x2 9.29 us: per_device(): lax.fori_loop(0, slot_count, reverse_visit, initial_state)]
  transfers between devices with their start and end apart: 19 -> 7, of which waited for: 7 -> 4; matrix products, arithmetic and copies ran while one was open for 18% -> 9% of each run, Pallas kernels for 0% -> 40%
where the time goes in v1:
time: 251 us; the launch traced here: 250 us
  waiting for transfers between devices  104 us (41%)
  Pallas kernels  101 us (40%)
  matrix products  19.8 us (8%)
  between operations  13.9 us (6%)
  other arithmetic  6.53 us (3%)
  local copies, waits for them, and re-layouts  3.77 us (2%)
    pallas_call x2, Pallas kernels, exchange(): pl.pallas_call(functools.partial(body, count), out_shape=(jax.ShapeDtypeS...  71.6 us
    reduce_scatter x1, waiting for transfers between devices, paired_device(): lax.psum_scatter(out_terms.astype(jnp.bfloat16), 'head', scatter_dimensio...  59.6 us
    all_gather x1, waiting for transfers between devices, paired_device(): piece = lax.all_gather(grad_out, 'head', axis=1, tiled=True)  33.7 us
    dot_general x3, matrix products, dot(): lax.dot_general(left, right, dims, preferred_element_type=jnp.float32)  19.8 us
    pallas_call x1, Pallas kernels, backward_units(): pl.pallas_call(backward_kernel, grid_spec=pltpu.PrefetchScalarGridSpec(nu...  16.7 us
    pallas_call x1, Pallas kernels, forward_units(): pl.pallas_call(forward_kernel, grid_spec=pltpu.PrefetchScalarGridSpec(num...  12.3 us
    ppermute x1, waiting for transfers between devices, to_units(): lax.ppermute(jnp.where(core == 0, second, first), 'ctx', [(c, c + 1) for...  6.68 us
  transfers between devices with their start and end apart: 7, of which 4 were waited for; matrix products, arithmetic and copies ran while one was open for 9% of the time, Pallas kernels for 40%

profile of v1, /device:TPU:0, one launch (start us, length us, event | category | flops | bytes accessed | tf_op | source)
XLA Modules:
  0.0 250.4 jit_solution(8683757109963957563)
XLA Ops:
  7.2 0.7 all-gather.2.cloned.1.call-update
  8.1 0.6 gather_fusion
  8.6 1.1 slice_bitcast_fusion.8
  9.7 1.1 slice_bitcast_fusion.10
  11.0 31.0 %shard_map.101 = (bf16[8,512,256]{2,1,0:T(8,128)(2,1)S(1)}, bf16[2,512,256]{2,1,0:T(8,128)(2,1)S(1)}) custom-call(bf16[2,512,256]{2,1,0:T(8,128)(2,1)S(1)} %maximum_maximum_fusion.kv_ref, bf16[2,512,256]{2,1,0:T(8,128)(2,1)S(1)} %pad_maximum_fusion.q_ref), custom_call_target="tpu_custom_call" | custom-call | bytes 2097152 | tf_op jit(solution)/shard_map/pallas_call | solution.py:333
  42.1 12.3 %shard_map.102 = (bf16[2,512,256]{2,1,0:T(8,128)(2,1)S(1)}, f32[2,2,512]{2,1,0:T(2,128)S(1)}) custom-call(s32[2,8]{1,0:T(2,128)S(1)} %broadcast_select_fusion.2.rows_ref, bf16[2,512,256]{2,1,0:T(8,128)(2,1)S(1)} %get-tuple-element.13.q_ref, bf16[8,512,256]{2,1,0:T(8,128)(2,1)S(1)} %get-tuple-element.14.kv_ref), custom_call_target="tpu_custom_call" | custom-call | flops 1342177280 | bytes 2097152 | tf_op jit(solution)/shard_map/pallas_call | solution.py:420
  54.6 0.7 collective-permute-start.1
  55.3 3.3 %collective-permute-done = bf16[512,256]{1,0:T(8,128)(2,1)S(1)} collective-permute-done((bf16[512,256]{1,0:T(8,128)(2,1)S(1)}, bf16[512,256]{1,0:T(8,128)(2,1)S(1)}, u32[]{:S(2)}, u32[]{:S(2)}) %collective-permute-start) | collective-permute-done | bytes 262176 | tf_op jit(solution)/shard_map/ppermute | solution.py:557
  58.6 0.7 bitcast_select_fusion
  59.4 33.7 %all-gather.2.cloned.1.call-done = bf16[512,4096]{1,0:T(8,128)(2,1)} async-done(((bf16[512,1024]{1,0:T(8,128)(2,1)}), bf16[512,4096]{1,0:T(8,128)(2,1)}) %all-gather.2.cloned.1.call-update) | async-done | bytes 4194320 | tf_op jit(solution)/shard_map/all_gather | solution.py:573
  93.1 6.6 %convolution_convert_fusion = bf16[512,4096]{1,0:T(8,128)(2,1)} fusion(bf16[512,4096]{1,0:T(8,128)(2,1)} %all-gather.2.cloned.1.call-done, bf16[512,256]{1,0:T(8,128)(2,1)} %get-tuple-element.32, bf16[512,256]{1,0:T(8,128)(2,1)S(1)} %get-tuple-element.31), kind=kOutput, calls=%fused_computation.1 | convolution fusion | flops 2150629376 | bytes 8912896 | tf_op jit(solution)/shard_map/dot_general | solution.py:234
  99.8 0.9 copy-done.2
  100.7 6.5 %convolution_convert_fusion.1 = bf16[512,4096]{1,0:T(8,128)(2,1)} fusion(bf16[512,4096]{1,0:T(8,128)(2,1)} %param.9, bf16[512,256]{1,0:T(8,128)(2,1)S(1)} %copy-done.2, bf16[512,256]{1,0:T(8,128)(2,1)S(1)} %get-tuple-element.31), kind=kOutput, calls=%fused_computation.2 | convolution fusion | flops 2150629376 | bytes 8912896 | tf_op jit(solution)/shard_map/dot_general | solution.py:234
  107.2 6.6 %convolution_convert_fusion.2 = bf16[512,512]{1,0:T(8,128)(2,1)S(1)} fusion(bf16[512,4096]{1,0:T(8,128)(2,1)} %all-gather.2.cloned.1.call-done, bf16[512,4096]{1,0:T(8,128)(2,1)} %param.9), kind=kOutput, calls=%fused_computation.4 | convolution fusion | flops 2147745792 | bytes 8912896 | tf_op jit(solution)/shard_map/dot_general | solution.py:234
  113.9 6.7 %collective-permute-done.2 = bf16[512,256]{1,0:T(8,128)(2,1)S(1)} collective-permute-done((bf16[512,256]{1,0:T(8,128)(2,1)S(1)}, bf16[512,256]{1,0:T(8,128)(2,1)S(1)}, u32[]{:S(2)}, u32[]{:S(2)}) %collective-permute-start.2) | collective-permute-done | bytes 262176 | tf_op jit(solution)/shard_map/ppermute | solution.py:546
  120.7 0.9 collective-permute-start.3
  121.6 16.7 %shard_map.103 = (bf16[2,512,256]{2,1,0:T(8,128)(2,1)S(1)}, bf16[8,512,256]{2,1,0:T(8,128)(2,1)S(1)}) custom-call(s32[2,8]{1,0:T(2,128)S(1)} %broadcast_select_fusion.2.rows_ref, bf16[2,512,256]{2,1,0:T(8,128)(2,1)S(1)} %get-tuple-element.13.q_ref, bf16[2,512,256]{2,1,0:T(8,128)(2,1)S(1)} %pad_maximum_fusion.2.g_ref, ...), custom_call_target="tpu_custom_call" | custom-call | flops 3355443200 | bytes 4194304 | tf_op jit(solution)/shard_map/pallas_call | solution.py:512
  138.4 40.6 %shard_map.104 = (bf16[8,512,256]{2,1,0:T(8,128)(2,1)S(1)}, bf16[2,512,256]{2,1,0:T(8,128)(2,1)S(1)}) custom-call(bf16[8,512,256]{2,1,0:T(8,128)(2,1)S(1)} %get-tuple-element.17.dkv_ref, bf16[2,512,256]{2,1,0:T(8,128)(2,1)S(1)} %get-tuple-element.18.dq_ref), custom_call_target="tpu_custom_call" | custom-call | bytes 5242880 | tf_op jit(solution)/shard_map/pallas_call | solution.py:333
  179.0 0.3 convert_reduce_fusion
  179.4 0.8 pad_maximum_fusion.4
  180.2 0.8 pad_maximum_fusion.3
  181.1 1.1 maximum_convert_fusion
  182.2 2.2 convert_element_type.27
  184.3 59.6 %reduce-scatter.3.cloned.1.call-done = bf16[512,1024]{1,0:T(8,128)(2,1)} async-done(((bf16[512,4096]{1,0:T(8,128)(2,1)}), bf16[512,1024]{1,0:T(8,128)(2,1)}) %reduce-scatter.3.cloned.1.call-update) | async-done | bytes 1048592 | tf_op jit(solution)/shard_map/reduce_scatter | solution.py:587
  (29 shorter events, 1.0 us)
Async XLA Ops:
  7.2 0.9 copy-start
  7.2 85.9 %all-gather.2.cloned.1.call-start = ((), (), s32[]{:S(2)}) async-start(), calls=%async_computation.3 | async-start | bytes 5242880 | tf_op jit(solution)/shard_map/all_gather | solution.py:573
  7.9 174.3 %reduce-scatter.5.cloned.1.call-start = ((), (), s32[]{:S(2)}) async-start(), calls=%async_computation.4 | async-start | bytes 4718592 | tf_op jit(solution)/shard_map/reduce_scatter | solution.py:593
  42.0 57.7 %copy-start.1 = (bf16[8,512,256]{2,1,0:T(8,128)(2,1)}, bf16[8,512,256]{2,1,0:T(8,128)(2,1)S(1)}, u32[]{:S(2)}) copy-start(bf16[8,512,256]{2,1,0:T(8,128)(2,1)S(1)} %get-tuple-element.14.kv_ref) | copy-start | bytes 6291460
  54.5 4.1 %collective-permute-start = (bf16[512,256]{1,0:T(8,128)(2,1)S(1)}, bf16[512,256]{1,0:T(8,128)(2,1)S(1)}, u32[]{:S(2)}, u32[]{:S(2)}) collective-permute-start(bf16[512,256]{1,0:T(8,128)(2,1)S(1)} %bitcast_select_fusion.1), channel_id=1, source_target_pairs={{0,28},{8,20},{16,12},{24,4},{4,0},{12,8},{20,16},{28,24},{1,29},{... | collective-permute-start | bytes 786440 | tf_op jit(solution)/shard_map/ppermute | solution.py:557
  54.6 4.0 %collective-permute-start.1 = (bf16[512,256]{1,0:T(8,128)(2,1)S(1)}, bf16[512,256]{1,0:T(8,128)(2,1)S(1)}, u32[]{:S(2)}, u32[]{:S(2)}) collective-permute-start(bf16[512,256]{1,0:T(8,128)(2,1)S(1)} %slice_bitcast_fusion.6), channel_id=1, source_target_pairs={{4,28},{12,20},{20,12},{28,4},{5,29},{13,21},{21,13},{29,5},{6,30}... | collective-permute-start | bytes 786440 | tf_op jit(solution)/shard_map/ppermute | solution.py:562
  99.7 1.0 copy-start.2
  99.7 144.2 %reduce-scatter.3.cloned.1.call-start = ((), (), s32[]{:S(2)}) async-start(), calls=%async_computation.2 | async-start | bytes 5242880 | tf_op jit(solution)/shard_map/reduce_scatter | solution.py:587
  113.9 6.7 %collective-permute-start.2 = (bf16[512,256]{1,0:T(8,128)(2,1)S(1)}, bf16[512,256]{1,0:T(8,128)(2,1)S(1)}, u32[]{:S(2)}, u32[]{:S(2)}) collective-permute-start(bf16[512,256]{1,0:T(8,128)(2,1)S(1)} %broadcast_select_fusion), channel_id=1, source_target_pairs={{0,4},{8,12},{16,20},{24,28},{4,24},{12,16},{20,8},{28,0},{1,5},{9... | collective-permute-start | bytes 786440 | tf_op jit(solution)/shard_map/ppermute | solution.py:546
  120.7 0.9 collective-permute-start.3
Sparse Core Ops, SparseCore 0:
  9.6 83.4 all-gather.1
  99.9 51.7 reduce-scatter.4
  154.6 89.2 reduce-scatter.2

commit v2 on v1

--- a/solution.py
+++ b/solution.py
@@ -252,89 +252,34 @@
     )
 
 
-def spread_kernel(count, kv_ref, q_ref, kv_all, q_units, send, recv, q_send, q_recv, local):
+def exchange_kernel(count, by_core, blocks_ref, halves_ref, blocks_all, other, send, recv, half, local):
     me = lax.axis_index("ctx")
     core = lax.rem(me, 2)
-    sibling = me + 1 - 2 * core
-    across = count - 2 - (me - core)
     greet([lax.rem(me + step, count) for step in range(1, count)], count - 1)
-    copies = []
+    source = halves_ref.at[1 - core] if by_core else halves_ref.at[1]
+    copies = [remote(source, other, half.at[0], half.at[1], count - 1 - me)]
+    copies[0].start()
     for step in range(1, count):
         peer = lax.rem(me + step, count)
-        copy = remote(
-            kv_ref.at[lax.rem(peer, 2)], kv_all.at[me], send.at[step], recv.at[step], peer
-        )
+        index = lax.rem(peer, 2) if by_core else peer
+        copy = remote(blocks_ref.at[index], blocks_all.at[me], send.at[step], recv.at[step], peer)
         copy.start()
         copies.append(copy)
-
-    @pl.when(core == 0)
-    def _():
-        remote(q_ref.at[1], q_units.at[0], q_send.at[0], q_recv.at[0], sibling).start()
-        mine = pltpu.make_async_copy(q_ref.at[0], q_units.at[0], local.at[1])
-        mine.start()
-        mine.wait()
-
-    @pl.when(core == 1)
-    def _():
-        remote(q_ref.at[0], q_units.at[1], q_send.at[0], q_recv.at[1], across).start()
-        remote(q_ref.at[1], q_units.at[1], q_send.at[1], q_recv.at[1], across + 1).start()
-
-    mine = pltpu.make_async_copy(kv_ref.at[core], kv_all.at[me], local.at[0])
+    index = core if by_core else me
+    mine = pltpu.make_async_copy(blocks_ref.at[index], blocks_all.at[me], local)
     mine.start()
     mine.wait()
     for copy in copies:
         copy.wait()
 
-    remote(q_ref.at[0], q_units.at[1], q_send.at[0], q_recv.at[1], across).wait()
-
-    @pl.when(core == 1)
-    def _():
-        remote(q_ref.at[1], q_units.at[0], q_send.at[1], q_recv.at[0], sibling).wait()
-
-
-def return_kernel(count, dkv_ref, dq_ref, dkv_all, dq_halves, send, recv, q_send, q_recv, local):
-    me = lax.axis_index("ctx")
-    core = lax.rem(me, 2)
-    sibling = me + 1 - 2 * core
-    across = count - 2 - (me - core)
-    greet([lax.rem(me + step, count) for step in range(1, count)], count - 1)
-    copies = []
-    for step in range(1, count):
-        peer = lax.rem(me + step, count)
-        copy = remote(dkv_ref.at[peer], dkv_all.at[me], send.at[step], recv.at[step], peer)
-        copy.start()
-        copies.append(copy)
-    remote(dq_ref.at[1], dq_halves.at[core], q_send.at[0], q_recv.at[core], across + 1).start()
-
-    @pl.when(core == 1)
-    def _():
-        remote(dq_ref.at[0], dq_halves.at[1], q_send.at[1], q_recv.at[1], sibling).start()
-
-    @pl.when(core == 0)
-    def _():
-        mine = pltpu.make_async_copy(dq_ref.at[0], dq_halves.at[0], local.at[1])
-        mine.start()
-        mine.wait()
-
-    mine = pltpu.make_async_copy(dkv_ref.at[me], dkv_all.at[me], local.at[0])
-    mine.start()
-    mine.wait()
-    for copy in copies:
-        copy.wait()
-    remote(dq_ref.at[1], dq_halves.at[1], q_send.at[0], q_recv.at[1], across + 1).wait()
-
-    @pl.when(core == 1)
-    def _():
-        remote(dq_ref.at[0], dq_halves.at[0], q_send.at[1], q_recv.at[0], across).wait()
-
-
-def exchange(body, collective_id, count, blocks, units):
+
+def exchange(by_core, collective_id, count, blocks, units):
     any_space = pl.BlockSpec(memory_space=pl.ANY)
     return pl.pallas_call(
-        functools.partial(body, count),
+        functools.partial(exchange_kernel, count, by_core),
         out_shape=(
             jax.ShapeDtypeStruct((count,) + blocks.shape[1:], blocks.dtype),
-            jax.ShapeDtypeStruct(units.shape, units.dtype),
+            jax.ShapeDtypeStruct(units.shape[1:], units.dtype),
         ),
         in_specs=[any_space, any_space],
         out_specs=(any_space, any_space),
@@ -342,8 +287,7 @@
             pltpu.SemaphoreType.DMA((count,)),
             pltpu.SemaphoreType.DMA((count,)),
             pltpu.SemaphoreType.DMA((2,)),
-            pltpu.SemaphoreType.DMA((2,)),
-            pltpu.SemaphoreType.DMA((2,)),
+            pltpu.SemaphoreType.DMA,
         ],
         compiler_params=pltpu.CompilerParams(
             collective_id=collective_id, has_side_effects=True, vmem_limit_bytes=VMEM_BYTES
@@ -540,62 +484,62 @@
     return jnp.stack([value[:, :half], value[:, half:]])
 
 
-def to_units(home, core, count):
-    first, second = home[0], home[1]
-    even = range(0, count, 2)
-    one = lax.ppermute(
-        jnp.where(core == 0, second, first),
-        "ctx",
-        [(c, c + 1) for c in even] + [(c + 1, count - 2 - c) for c in even],
-    )
-    two = lax.ppermute(second, "ctx", [(c + 1, count - 1 - c) for c in even])
-    return jnp.stack([jnp.where(core == 0, first, one), jnp.where(core == 0, one, two)])
-
-
-def to_home(units, core, count):
-    even = range(0, count, 2)
-    one = lax.ppermute(
-        jnp.where(core == 0, units[1], units[0]),
-        "ctx",
-        [(c, count - 1 - c) for c in even] + [(c + 1, c) for c in even],
-    )
-    two = lax.ppermute(units[1], "ctx", [(c + 1, count - 1 - c) for c in even])
-    return jnp.concatenate(
-        [jnp.where(core == 0, units[0], one), jnp.where(core == 0, one, two)], 1
-    )
+def swapped(value, count):
+    return lax.ppermute(value, "ctx", [(c, count - 1 - c) for c in range(count)])
+
+
+def merged_cores(terms, core, count):
+    tiles = terms.reshape(count // 2, 2, terms.shape[0] // count, terms.shape[1])
+    kept = jnp.where(core == 0, tiles[:, 0], tiles[:, 1])
+    given = jnp.where(core == 0, tiles[:, 1], tiles[:, 0])
+    taken = lax.ppermute(given, "ctx", [(c, c ^ 1) for c in range(count)])
+    return (kept.astype(jnp.float32) + taken.astype(jnp.float32)).astype(jnp.bfloat16)
 
 
 def paired_device(query_proj, projected_keys, projected_values, w_out, attended_blocks, grad_out):
     count = lax.axis_size("ctx")
     me = lax.axis_index("ctx")
-    core = lax.rem(me, 2)
+    core, chip = lax.rem(me, 2), lax.div(me, 2)
     tokens = query_proj.shape[0]
     piece = lax.all_gather(grad_out, "head", axis=1, tiled=True)
     key_halves, value_halves = halves_of(projected_keys), halves_of(projected_values)
-    kv_all, q_units = exchange(
-        spread_kernel,
-        0,
-        count,
-        jnp.concatenate([key_halves, value_halves], 2),
-        halves_of(query_proj),
-    )
-    own_even = me - core
-    rows = jnp.take(attended_blocks, jnp.stack([own_even, count - 1 - own_even]), axis=0)
+
+    def own_half(halves):
+        return jnp.where(core == 0, halves[0], halves[1])
+
+    def both_halves(own, other):
+        return jnp.concatenate(
+            [jnp.where(core == 0, own, other), jnp.where(core == 0, other, own)], 1
+        )
+
+    query_halves = halves_of(query_proj)
+    kv_all, q_other = exchange(
+        True, 0, count, jnp.concatenate([key_halves, value_halves], 2), query_halves
+    )
+    q_units = jnp.stack([own_half(query_halves), q_other])
+    rows = jnp.take(attended_blocks, jnp.stack([me, count - 1 - me]), axis=0)
     attn_units, totals = forward_units(rows, q_units, kv_all)
-    attn = to_home(attn_units, core, count)
-    out_terms = dot(attn, w_out)
-    layer_out = lax.psum_scatter(
-        out_terms.astype(jnp.bfloat16), "head", scatter_dimension=1, tiled=True
-    )
-    grad_attn = dot(piece, w_out, CONTRACT_LAST).astype(jnp.bfloat16)
-    g_units = to_units(halves_of(grad_attn), core, count)
-    weight_terms = dot(attn, piece, CONTRACT_FIRST)
-    grad_wout = lax.psum_scatter(
-        weight_terms.astype(jnp.bfloat16), "ctx", scatter_dimension=1, tiled=True
-    ).astype(jnp.float32)
+    attn = both_halves(attn_units[0], swapped(attn_units[1], count))
+    out_terms = dot(attn, w_out).astype(jnp.bfloat16)
+    piece, out_terms = lax.optimization_barrier((piece, out_terms))
+    layer_out = lax.psum_scatter(out_terms, "head", scatter_dimension=1, tiled=True)
+    merged = merged_cores(dot(piece, attn, CONTRACT_FIRST).astype(jnp.bfloat16), core, count)
+    grad_halves = halves_of(dot(piece, w_out, CONTRACT_LAST).astype(jnp.bfloat16))
+    grad_other = swapped(own_half(grad_halves[::-1]), count)
+    g_units = jnp.stack([own_half(grad_halves), grad_other])
+    merged, g_units = lax.optimization_barrier((merged, g_units))
+    parts = []
+    for turn in range(1, count // 2):
+        part = lax.dynamic_index_in_dim(merged, chip ^ turn, 0, keepdims=False)
+        parts.append(lax.ppermute(part, "ctx", [(c, c ^ (2 * turn)) for c in range(count)]))
     dq_units, dkv = backward_units(rows, q_units, g_units, attn_units, totals, kv_all)
-    dkv_all, dq_halves = exchange(return_kernel, 1, count, dkv, dq_units)
-    grad_query = jnp.concatenate([dq_halves[0], dq_halves[1]], 1).astype(jnp.float32)
+    parts, dq_units, dkv = lax.optimization_barrier((parts, dq_units, dkv))
+    dkv_all, dq_other = exchange(False, 1, count, dkv, dq_units)
+    total = lax.dynamic_index_in_dim(merged, chip, 0, keepdims=False).astype(jnp.float32)
+    for part in parts:
+        total = total + part.astype(jnp.float32)
+    grad_wout = total.T
+    grad_query = both_halves(dq_units[0], dq_other).astype(jnp.float32)
     summed = jnp.sum(
         dkv_all.reshape(count // 2, 2, tokens, 2 * HEAD_SIZE).astype(jnp.float32), 0
     )
@@ -609,7 +553,8 @@
     pairs = (
         projected_keys.shape[1] == 2 * HEAD_SIZE
         and query_proj.shape[0] == BLOCK_TOKENS
-        and count % 4 == 0
+        and count >= 4
+        and count & (count - 1) == 0
         and attended_blocks.shape[1] >= count
     )
     body = paired_device if pairs else general_device

time: 251 us -> 200 us (0.80)
  waiting for transfers between devices: 104 us -> 40.9 us
  local copies, waits for them, and re-layouts: 3.77 us -> 14.5 us
  Pallas kernels: 101 us -> 92.7 us
  starting transfers between devices: 1.77 us -> 9.43 us
  other arithmetic: 6.53 us -> 13.9 us
  matrix products: 19.8 us -> 13.4 us
    reduce_scatter x2 -> x1, waiting for transfers between devices: 59.6 us -> 0.01 us  [paired_device(): lax.psum_scatter(out_terms, 'head', scatter_dimension=1, tiled=True)]
    all_gather x1, waiting for transfers between devices: 33.7 us -> 23.6 us  [paired_device(): piece = lax.all_gather(grad_out, 'head', axis=1, tiled=True)]
    unnamed x6 -> x14, local copies, waits for them, and re-layouts: 0.89 us -> 10.3 us
    pallas_call x2, Pallas kernels: 71.6 us -> 63.4 us  [exchange(): pl.pallas_call(functools.partial(exchange_kernel, count, by_core), out_sh...]
    ppermute x4 -> x6, starting transfers between devices: 1.65 us -> 9.35 us  [the longest x2 5.8 us: swapped(): lax.ppermute(value, 'ctx', [(c, count - 1 - c) for c in range(count)])]
    ppermute x4 -> x6, waiting for transfers between devices: 10 us -> 16.7 us  [the longest x2 10.5 us: swapped(): lax.ppermute(value, 'ctx', [(c, count - 1 - c) for c in range(count)])]
    dot_general x3, matrix products: 19.8 us -> 13.4 us  [dot(): lax.dot_general(left, right, dims, preferred_element_type=jnp.float32)]
    transpose x0 -> x1, other arithmetic: none -> 2.75 us  [paired_device(): grad_wout = total.T]
  transfers between devices with their start and end apart: 7 -> 8, of which waited for: 4 -> 4; matrix products, arithmetic and copies ran while one was open for 9% -> 20% of each run, Pallas kernels for 40% -> 47%
where the time goes in v2:
time: 200 us; the launch traced here: 199 us
  Pallas kernels  92.7 us (46%)
  waiting for transfers between devices  40.9 us (20%)
  local copies, waits for them, and re-layouts  14.5 us (7%)
  between operations  14.3 us (7%)
  other arithmetic  13.9 us (7%)
  matrix products  13.4 us (7%)
  starting transfers between devices  9.43 us (5%)
    pallas_call x2, Pallas kernels, exchange(): pl.pallas_call(functools.partial(exchange_kernel, count, by_core), out_sh...  63.4 us
    all_gather x1, waiting for transfers between devices, paired_device(): piece = lax.all_gather(grad_out, 'head', axis=1, tiled=True)  23.6 us
    pallas_call x1, Pallas kernels, backward_units(): pl.pallas_call(backward_kernel, grid_spec=pltpu.PrefetchScalarGridSpec(nu...  16.9 us
    dot_general x3, matrix products, dot(): lax.dot_general(left, right, dims, preferred_element_type=jnp.float32)  13.4 us
    pallas_call x1, Pallas kernels, forward_units(): pl.pallas_call(forward_kernel, grid_spec=pltpu.PrefetchScalarGridSpec(num...  12.4 us
    ppermute x2, waiting for transfers between devices, swapped(): lax.ppermute(value, 'ctx', [(c, count - 1 - c) for c in range(count)])  10.5 us
    unnamed x14, local copies, waits for them, and re-layouts  10.3 us
    ppermute x3, waiting for transfers between devices, paired_device(): lax.ppermute(part, 'ctx', [(c, c ^ 2 * turn) for c in range(count)])  6.21 us
  transfers between devices with their start and end apart: 8, of which 4 were waited for; matrix products, arithmetic and copies ran while one was open for 20% of the time, Pallas kernels for 47%

profile of v2, /device:TPU:0, one launch (start us, length us, event | category | flops | bytes accessed | tf_op | source)
XLA Modules:
  0.0 199.0 jit_solution(8146453781908252512)
XLA Ops:
  9.8 1.1 slice_bitcast_fusion.8
  11.0 32.8 %shard_map.101 = (bf16[8,512,256]{2,1,0:T(8,128)(2,1)S(1)}, bf16[512,256]{1,0:T(8,128)(2,1)S(1)}) custom-call(bf16[2,512,256]{2,1,0:T(8,128)(2,1)S(1)} %maximum_maximum_fusion.blocks_ref, bf16[2,512,256]{2,1,0:T(8,128)(2,1)S(1)} %pad_maximum_fusion.halves_ref), custom_call_target="tpu_custom_call" | custom-call | bytes 2097152 | tf_op jit(solution)/shard_map/pallas_call | solution.py:278
  44.0 12.4 %shard_map.102 = (bf16[2,512,256]{2,1,0:T(8,128)(2,1)S(1)}, f32[2,2,512]{2,1,0:T(2,128)S(1)}) custom-call(s32[2,8]{1,0:T(2,128)S(1)} %broadcast_select_fusion.1.rows_ref, bf16[2,512,256]{2,1,0:T(8,128)(2,1)S(1)} %pad_maximum_fusion.1.q_ref, bf16[8,512,256]{2,1,0:T(8,128)(2,1)S(1)} %get-tuple-element.23.kv_ref), custom_call_target="tpu_custom_call" | custom-call | flops 1342177280 | bytes 2097152 | tf_op jit(solution)/shard_map/pallas_call | solution.py:364
  56.4 1.4 copy-done.1
  57.8 3.3 %collective-permute-start = (bf16[512,256]{1,0:T(8,128)(2,1)S(1)}, bf16[512,256]{1,0:T(8,128)(2,1)S(1)}, u32[]{:S(2)}, u32[]{:S(2)}) collective-permute-start(bf16[512,256]{1,0:T(8,128)(2,1)S(1)} %slice_bitcast_fusion.4), channel_id=1, source_target_pairs={{0,28},{4,24},{8,20},{12,16},{16,12},{20,8},{24,4},{28,0},{1,29},{... | collective-permute-start | bytes 786440 | tf_op jit(solution)/shard_map/ppermute | solution.py:488
  61.1 4.1 %collective-permute-done = bf16[512,256]{1,0:T(8,128)(2,1)S(1)} collective-permute-done((bf16[512,256]{1,0:T(8,128)(2,1)S(1)}, bf16[512,256]{1,0:T(8,128)(2,1)S(1)}, u32[]{:S(2)}, u32[]{:S(2)}) %collective-permute-start) | collective-permute-done | bytes 262176 | tf_op jit(solution)/shard_map/ppermute | solution.py:488
  65.2 4.3 %convolution_convert_fusion.1 = bf16[512,4096]{1,0:T(8,128)(2,1)} fusion(bf16[512,4096]{1,0:T(8,128)(2,1)S(1)} %copy-done.4, bf16[512,256]{1,0:T(8,128)(2,1)S(1)} %get-tuple-element.51, bf16[512,256]{1,0:T(8,128)(2,1)S(1)} %get-tuple-element.50), kind=kOutput, calls=%fused_computation.2 | convolution fusion | flops 2150629376 | bytes 8912896 | tf_op jit(solution)/shard_map/dot_general | solution.py:234
  69.5 23.6 %all-gather.2.cloned.1.call-done = bf16[512,4096]{1,0:T(8,128)(2,1)} async-done(((bf16[512,1024]{1,0:T(8,128)(2,1)}), bf16[512,4096]{1,0:T(8,128)(2,1)}) %all-gather.2.cloned.1.call-update) | async-done | bytes 4194320 | tf_op jit(solution)/shard_map/all_gather | solution.py:504
  93.1 4.6 %convolution_convert_fusion = bf16[4096,512]{1,0:T(8,128)(2,1)S(1)} fusion(bf16[512,4096]{1,0:T(8,128)(2,1)} %all-gather.2.cloned.1.call-done, bf16[512,256]{1,0:T(8,128)(2,1)S(1)} %get-tuple-element.51, bf16[512,256]{1,0:T(8,128)(2,1)S(1)} %get-tuple-element.50), kind=kOutput, calls=%fused_computation.1 | convolution fusion | flops 2150629376 | bytes 8912896 | tf_op jit(solution)/shard_map/dot_general | solution.py:234
  97.7 2.2 %fusion.7 = (bf16[4,1,512,512]{3,2,1,0:T(8,128)(2,1)}, bf16[4,1,512,512]{3,2,1,0:T(8,128)(2,1)}) fusion(bf16[4,2,512,512]{3,2,1,0:T(8,128)(2,1)S(1)} %bitcast.65), kind=kLoop, calls=%fused_computation.49 | loop fusion | bytes 8388608 | tf_op jit(solution)/shard_map/slice | solution.py:493
  99.9 3.0 %copy.13 = bf16[4,1,512,512]{2,3,0,1:T(8,128)(2,1)S(1)} copy(bf16[4,1,512,512]{3,2,1,0:T(8,128)(2,1)} %get-tuple-element.39) | data formatting | bytes 4194304
  103.0 4.6 %copy.14 = bf16[4,1,512,512]{2,3,0,1:T(8,128)(2,1)} copy(bf16[4,1,512,512]{3,2,1,0:T(8,128)(2,1)} %get-tuple-element.40) | data formatting | bytes 4194304
  107.5 3.3 %select_bitcast_fusion = bf16[4,512,512]{1,2,0:T(8,128)(2,1)} fusion(bf16[4,1,512,512]{2,3,0,1:T(8,128)(2,1)} %copy.14, bf16[4,1,512,512]{2,3,0,1:T(8,128)(2,1)S(1)} %copy.13, pred[]{:T(512)S(6)} %eq.2), kind=kLoop, calls=%fused_computation.6 | loop fusion | flops 1048576 | bytes 6291457 | tf_op jit(solution)/shard_map/jit(_where)/select_n | solution.py:494
  110.8 4.5 %convolution_convert_fusion.2 = bf16[512,512]{1,0:T(8,128)(2,1)S(1)} fusion(bf16[512,4096]{1,0:T(8,128)(2,1)} %all-gather.2.cloned.1.call-done, bf16[512,4096]{1,0:T(8,128)(2,1)S(1)} %copy-done.5), kind=kOutput, calls=%fused_computation.7 | convolution fusion | flops 2147745792 | bytes 8912896 | tf_op jit(solution)/shard_map/dot_general | solution.py:234
  115.4 2.5 %collective-permute-start.2 = (bf16[512,256]{1,0:T(8,128)(2,1)S(1)}, bf16[512,256]{1,0:T(8,128)(2,1)S(1)}, u32[]{:S(2)}, u32[]{:S(2)}) collective-permute-start(bf16[512,256]{1,0:T(8,128)(2,1)S(1)} %get-tuple-element.53), channel_id=1, source_target_pairs={{0,28},{4,24},{8,20},{12,16},{16,12},{20,8},{24,4},{28,0},{1,29},{... | collective-permute-start | bytes 786440 | tf_op jit(solution)/shard_map/ppermute | solution.py:488
  118.0 6.4 %collective-permute-done.2 = bf16[512,256]{1,0:T(8,128)(2,1)S(1)} collective-permute-done((bf16[512,256]{1,0:T(8,128)(2,1)S(1)}, bf16[512,256]{1,0:T(8,128)(2,1)S(1)}, u32[]{:S(2)}, u32[]{:S(2)}) %collective-permute-start.2) | collective-permute-done | bytes 262176 | tf_op jit(solution)/shard_map/ppermute | solution.py:488
  124.4 3.1 %fusion = bf16[4,512,512]{1,2,0:T(8,128)(2,1)S(1)} fusion(bf16[4,512,512]{1,2,0:T(8,128)(2,1)} %collective-permute-done.1, bf16[4,1,512,512]{2,3,0,1:T(8,128)(2,1)} %copy-done.2, bf16[4,1,512,512]{2,3,0,1:T(8,128)(2,1)} %copy.14, pred[]{:T(512)S(6)} %eq.2), kind=kLoop, calls=%fused_computation.5 | loop fusion | flops 5242880 | bytes 8388609 | tf_op jit(solution)/shard_map/convert_element_type | solution.py:496
  127.5 1.3 copy-done.3
  129.0 2.4 %collective-permute-start.5 = (bf16[512,512]{0,1:T(8,128)(2,1)S(1)}, bf16[512,512]{0,1:T(8,128)(2,1)}, u32[]{:S(2)}, u32[]{:S(2)}) collective-permute-start(bf16[512,512]{0,1:T(8,128)(2,1)S(1)} %get-tuple-element.41), channel_id=1, source_target_pairs={{0,24},{4,28},{8,16},{12,20},{16,8},{20,12},{24,0},{28,4},{1,25},{... | collective-permute-start | bytes 1572872 | tf_op jit(solution)/shard_map/ppermute | solution.py:534
  132.5 16.9 %shard_map.103 = (bf16[2,512,256]{2,1,0:T(8,128)(2,1)S(1)}, bf16[8,512,256]{2,1,0:T(8,128)(2,1)S(1)}) custom-call(s32[2,8]{1,0:T(2,128)S(1)} %broadcast_select_fusion.1.rows_ref, bf16[2,512,256]{2,1,0:T(8,128)(2,1)S(1)} %pad_maximum_fusion.1.q_ref, bf16[2,512,256]{2,1,0:T(8,128)(2,1)S(1)} %pad_maximum_fusion.3.g_ref, ...), custom_call_target="tpu_custom_call" | custom-call | flops 3355443200 | bytes 4194304 | tf_op jit(solution)/shard_map/pallas_call | solution.py:456
  149.4 6.2 %collective-permute-done.4 = bf16[512,512]{0,1:T(8,128)(2,1)} collective-permute-done((bf16[512,512]{0,1:T(8,128)(2,1)S(1)}, bf16[512,512]{0,1:T(8,128)(2,1)}, u32[]{:S(2)}, u32[]{:S(2)}) %collective-permute-start.4) | collective-permute-done | bytes 524320 | tf_op jit(solution)/shard_map/ppermute | solution.py:534
  155.6 30.6 %shard_map.104 = (bf16[8,512,256]{2,1,0:T(8,128)(2,1)S(1)}, bf16[512,256]{1,0:T(8,128)(2,1)S(1)}) custom-call(bf16[8,512,256]{2,1,0:T(8,128)(2,1)S(1)} %get-tuple-element.33.blocks_ref, bf16[2,512,256]{2,1,0:T(8,128)(2,1)S(1)} %get-tuple-element.32.halves_ref), custom_call_target="tpu_custom_call" | custom-call | bytes 5242880 | tf_op jit(solution)/shard_map/pallas_call | solution.py:278
  188.3 1.1 maximum_convert_fusion
  189.4 2.7 %fusion.3 = f32[512,512]{1,0:T(8,128)} fusion(bf16[512,512]{0,1:T(8,128)(2,1)} %collective-permute-done.5, bf16[512,512]{0,1:T(8,128)(2,1)} %collective-permute-done.4, bf16[512,512]{0,1:T(8,128)(2,1)} %collective-permute-done.3, bf16[4,512,512]{1,2,0:T(8,128)(2,1)} %copy-done.3, s32[]{:T(128)S(6)} %select_n.99), kind=kLoop, calls=%fused_computation.11 | loop fusion | flops 1835008 | bytes 3145732 | tf_op jit(solution)/shard_map/transpose | solution.py:541
  (40 shorter events, 6.4 us)
Async XLA Ops:
  7.2 0.9 copy-start
  7.2 85.9 %all-gather.2.cloned.1.call-start = ((), (), s32[]{:S(2)}) async-start(), calls=%async_computation.1 | async-start | bytes 5242880 | tf_op jit(solution)/shard_map/all_gather | solution.py:504
  7.9 184.3 %reduce-scatter.2.cloned.1.call-start = ((), (), s32[]{:S(2)}) async-start(), calls=%async_computation.2 | async-start | bytes 5242880 | tf_op jit(solution)/shard_map/reduce_scatter | solution.py:525
  11.0 54.2 %copy-start.4 = (bf16[512,4096]{1,0:T(8,128)(2,1)S(1)}, bf16[512,4096]{1,0:T(8,128)(2,1)}, u32[]{:S(2)}) copy-start(bf16[512,4096]{1,0:T(8,128)(2,1)} %param.9) | copy-start | bytes 12582916
  56.4 1.4 copy-start.1
  57.8 7.3 %collective-permute-start = (bf16[512,256]{1,0:T(8,128)(2,1)S(1)}, bf16[512,256]{1,0:T(8,128)(2,1)S(1)}, u32[]{:S(2)}, u32[]{:S(2)}) collective-permute-start(bf16[512,256]{1,0:T(8,128)(2,1)S(1)} %slice_bitcast_fusion.4), channel_id=1, source_target_pairs={{0,28},{4,24},{8,20},{12,16},{16,12},{20,8},{24,4},{28,0},{1,29},{... | collective-permute-start | bytes 786440 | tf_op jit(solution)/shard_map/ppermute | solution.py:488
  102.9 7.9 %copy-start.2 = (bf16[4,1,512,512]{2,3,0,1:T(8,128)(2,1)}, bf16[4,1,512,512]{2,3,0,1:T(8,128)(2,1)S(1)}, u32[]{:S(2)}) copy-start(bf16[4,1,512,512]{2,3,0,1:T(8,128)(2,1)S(1)} %copy.13) | copy-start | bytes 6291460
  107.5 3.3 %copy-start.5 = (bf16[512,4096]{1,0:T(8,128)(2,1)S(1)}, bf16[512,4096]{1,0:T(8,128)(2,1)}, u32[]{:S(2)}) copy-start(bf16[512,4096]{1,0:T(8,128)(2,1)} %param.9) | copy-start | bytes 12582916
  110.8 13.6 %collective-permute-start.1 = (bf16[4,512,512]{1,2,0:T(8,128)(2,1)}, bf16[4,512,512]{1,2,0:T(8,128)(2,1)}, u32[]{:S(2)}, u32[]{:S(2)}) collective-permute-start(bf16[4,512,512]{1,2,0:T(8,128)(2,1)} %select_bitcast_fusion), channel_id=1, source_target_pairs={{0,4},{4,0},{8,12},{12,8},{16,20},{20,16},{24,28},{28,24},{1,5},{5... | collective-permute-start | bytes 6291464 | tf_op jit(solution)/shard_map/ppermute | solution.py:495
  115.4 8.9 %collective-permute-start.2 = (bf16[512,256]{1,0:T(8,128)(2,1)S(1)}, bf16[512,256]{1,0:T(8,128)(2,1)S(1)}, u32[]{:S(2)}, u32[]{:S(2)}) collective-permute-start(bf16[512,256]{1,0:T(8,128)(2,1)S(1)} %get-tuple-element.53), channel_id=1, source_target_pairs={{0,28},{4,24},{8,20},{12,16},{16,12},{20,8},{24,4},{28,0},{1,29},{... | collective-permute-start | bytes 786440 | tf_op jit(solution)/shard_map/ppermute | solution.py:488
  127.5 1.3 copy-start.3
  129.0 20.4 %collective-permute-start.5 = (bf16[512,512]{0,1:T(8,128)(2,1)S(1)}, bf16[512,512]{0,1:T(8,128)(2,1)}, u32[]{:S(2)}, u32[]{:S(2)}) collective-permute-start(bf16[512,512]{0,1:T(8,128)(2,1)S(1)} %get-tuple-element.41), channel_id=1, source_target_pairs={{0,24},{4,28},{8,16},{12,20},{16,8},{20,12},{24,0},{28,4},{1,25},{... | collective-permute-start | bytes 1572872 | tf_op jit(solution)/shard_map/ppermute | solution.py:534
  131.4 24.2 %collective-permute-start.4 = (bf16[512,512]{0,1:T(8,128)(2,1)S(1)}, bf16[512,512]{0,1:T(8,128)(2,1)}, u32[]{:S(2)}, u32[]{:S(2)}) collective-permute-start(bf16[512,512]{0,1:T(8,128)(2,1)S(1)} %get-tuple-element.42), channel_id=1, source_target_pairs={{0,16},{4,20},{8,24},{12,28},{16,0},{20,4},{24,8},{28,12},{1,17},{... | collective-permute-start | bytes 1572872 | tf_op jit(solution)/shard_map/ppermute | solution.py:534
  132.0 23.7 %collective-permute-start.3 = (bf16[512,512]{0,1:T(8,128)(2,1)S(1)}, bf16[512,512]{0,1:T(8,128)(2,1)}, u32[]{:S(2)}, u32[]{:S(2)}) collective-permute-start(bf16[512,512]{0,1:T(8,128)(2,1)S(1)} %get-tuple-element.43), channel_id=1, source_target_pairs={{0,8},{4,12},{8,0},{12,4},{16,24},{20,28},{24,16},{28,20},{1,9},{5... | collective-permute-start | bytes 1572872 | tf_op jit(solution)/shard_map/ppermute | solution.py:534
Sparse Core Ops, SparseCore 0:
  9.6 83.4 all-gather.1
  95.9 75.2 reduce-scatter.1

commit v3 on v2

--- a/solution.py
+++ b/solution.py
@@ -496,12 +496,51 @@
     return (kept.astype(jnp.float32) + taken.astype(jnp.float32)).astype(jnp.bfloat16)
 
 
+def chip_parts(merged, chip, count):
+    parts = []
+    for turn in range(1, count // 2):
+        part = lax.dynamic_index_in_dim(merged, chip ^ turn, 0, keepdims=False)
+        parts.append(lax.ppermute(part, "ctx", [(c, c ^ (2 * turn)) for c in range(count)]))
+    return parts
+
+
+def sum_kernel(*refs):
+    out_ref = refs[-1]
+    width = refs[0].shape[0]
+    per_chunk = (len(refs) - 1) // (out_ref.shape[1] // width)
+    for chunk in range(out_ref.shape[1] // width):
+        total = refs[chunk * per_chunk][...].astype(jnp.float32)
+        for ref in refs[chunk * per_chunk + 1 : (chunk + 1) * per_chunk]:
+            total += ref[...].astype(jnp.float32)
+        out_ref[:, chunk * width : (chunk + 1) * width] = total.T
+
+
+def summed_chunks(chunks):
+    width, rows = chunks[0][0].shape
+    flat = [term for chunk in chunks for term in chunk]
+    return pl.pallas_call(
+        sum_kernel,
+        out_shape=jax.ShapeDtypeStruct((rows, width * len(chunks)), jnp.float32),
+        compiler_params=pltpu.CompilerParams(vmem_limit_bytes=VMEM_BYTES),
+    )(*flat)
+
+
+def column_chunk(value, tiles, chunk):
+    width = value.shape[1] // tiles // 2
+    starts = [(2 * tile + chunk) * width for tile in range(tiles)]
+    return jnp.concatenate([value[:, start : start + width] for start in starts], 1)
+
+
 def paired_device(query_proj, projected_keys, projected_values, w_out, attended_blocks, grad_out):
-    count = lax.axis_size("ctx")
+    count, groups = lax.axis_size("ctx"), lax.axis_size("head")
     me = lax.axis_index("ctx")
     core, chip = lax.rem(me, 2), lax.div(me, 2)
     tokens = query_proj.shape[0]
-    piece = lax.all_gather(grad_out, "head", axis=1, tiled=True)
+    own_tiles = count // groups
+    pieces = [
+        lax.all_gather(column_chunk(grad_out, own_tiles, chunk), "head", axis=1, tiled=True)
+        for chunk in range(2)
+    ]
     key_halves, value_halves = halves_of(projected_keys), halves_of(projected_values)
 
     def own_half(halves):
@@ -512,33 +551,44 @@
             [jnp.where(core == 0, own, other), jnp.where(core == 0, other, own)], 1
         )
 
+    def weight_terms(piece, attn):
+        terms = dot(piece, attn, CONTRACT_FIRST).astype(jnp.bfloat16)
+        return merged_cores(terms, core, count)
+
     query_halves = halves_of(query_proj)
     kv_all, q_other = exchange(
         True, 0, count, jnp.concatenate([key_halves, value_halves], 2), query_halves
     )
+    weights = [column_chunk(w_out, count, chunk) for chunk in range(2)]
     q_units = jnp.stack([own_half(query_halves), q_other])
     rows = jnp.take(attended_blocks, jnp.stack([me, count - 1 - me]), axis=0)
     attn_units, totals = forward_units(rows, q_units, kv_all)
     attn = both_halves(attn_units[0], swapped(attn_units[1], count))
     out_terms = dot(attn, w_out).astype(jnp.bfloat16)
-    piece, out_terms = lax.optimization_barrier((piece, out_terms))
+    first_merged = weight_terms(pieces[0], attn)
+    first_grad = dot(pieces[0], weights[0], CONTRACT_LAST)
+    first_parts = chip_parts(first_merged, chip, count)
+    last_piece, out_terms, first_parts, first_grad = lax.optimization_barrier(
+        (pieces[1], out_terms, first_parts, first_grad)
+    )
     layer_out = lax.psum_scatter(out_terms, "head", scatter_dimension=1, tiled=True)
-    merged = merged_cores(dot(piece, attn, CONTRACT_FIRST).astype(jnp.bfloat16), core, count)
-    grad_halves = halves_of(dot(piece, w_out, CONTRACT_LAST).astype(jnp.bfloat16))
+    grad_attn = first_grad + dot(last_piece, weights[1], CONTRACT_LAST)
+    grad_halves = halves_of(grad_attn.astype(jnp.bfloat16))
     grad_other = swapped(own_half(grad_halves[::-1]), count)
     g_units = jnp.stack([own_half(grad_halves), grad_other])
-    merged, g_units = lax.optimization_barrier((merged, g_units))
-    parts = []
-    for turn in range(1, count // 2):
-        part = lax.dynamic_index_in_dim(merged, chip ^ turn, 0, keepdims=False)
-        parts.append(lax.ppermute(part, "ctx", [(c, c ^ (2 * turn)) for c in range(count)]))
+    last_merged = weight_terms(last_piece, attn)
+    last_merged, g_units = lax.optimization_barrier((last_merged, g_units))
+    last_parts = chip_parts(last_merged, chip, count)
     dq_units, dkv = backward_units(rows, q_units, g_units, attn_units, totals, kv_all)
-    parts, dq_units, dkv = lax.optimization_barrier((parts, dq_units, dkv))
+    last_parts, dq_units, dkv = lax.optimization_barrier((last_parts, dq_units, dkv))
     dkv_all, dq_other = exchange(False, 1, count, dkv, dq_units)
-    total = lax.dynamic_index_in_dim(merged, chip, 0, keepdims=False).astype(jnp.float32)
-    for part in parts:
-        total = total + part.astype(jnp.float32)
-    grad_wout = total.T
+
+    def kept(merged):
+        return lax.dynamic_index_in_dim(merged, chip, 0, keepdims=False)
+
+    grad_wout = summed_chunks(
+        [[kept(first_merged)] + first_parts, [kept(last_merged)] + last_parts]
+    )
     grad_query = both_halves(dq_units[0], dq_other).astype(jnp.float32)
     summed = jnp.sum(
         dkv_all.reshape(count // 2, 2, tokens, 2 * HEAD_SIZE).astype(jnp.float32), 0
@@ -549,12 +599,14 @@
 
 
 def per_device(query_proj, projected_keys, projected_values, w_out, attended_blocks, grad_out):
-    count = lax.axis_size("ctx")
+    count, groups = lax.axis_size("ctx"), lax.axis_size("head")
     pairs = (
         projected_keys.shape[1] == 2 * HEAD_SIZE
         and query_proj.shape[0] == BLOCK_TOKENS
         and count >= 4
         and count & (count - 1) == 0
+        and groups & (groups - 1) == 0
+        and count % groups == 0
         and attended_blocks.shape[1] >= count
     )
     body = paired_device if pairs else general_device

time: 200 us -> 194 us (0.970)
  waiting for transfers between devices: 40.9 us -> 21.6 us
  local copies, waits for them, and re-layouts: 14.5 us -> 23.9 us
  matrix products: 13.4 us -> 18.2 us
  other arithmetic: 13.9 us -> 9.61 us
  starting transfers between devices: 9.43 us -> 12.4 us
    all_gather x1 -> x2, waiting for transfers between devices: 23.6 us -> 9.54 us  [paired_device(): lax.all_gather(column_chunk(grad_out, own_tiles, chunk), 'head', axis=1,...]
    unnamed x14 -> x29, local copies, waits for them, and re-layouts: 10.3 us -> 19 us
    ppermute x3 -> x6, waiting for transfers between devices: 6.21 us -> 0.02 us  [chip_parts(): lax.ppermute(part, 'ctx', [(c, c ^ 2 * turn) for c in range(count)])]
    dot_general x3 -> x5, matrix products: 13.4 us -> 18.2 us  [dot(): lax.dot_general(left, right, dims, preferred_element_type=jnp.float32)]
    reduce_scatter x1, waiting for transfers between devices: 0.01 us -> 4.22 us  [paired_device(): lax.psum_scatter(out_terms, 'head', scatter_dimension=1, tiled=True)]
    ppermute x3 -> x6, starting transfers between devices: 3.55 us -> 7.04 us  [chip_parts(): lax.ppermute(part, 'ctx', [(c, c ^ 2 * turn) for c in range(count)])]
    transpose x1 -> x0, other arithmetic: 2.75 us -> none  [paired_device(): grad_wout = total.T]
    ppermute x2, waiting for transfers between devices: 10.5 us -> 7.79 us  [swapped(): lax.ppermute(value, 'ctx', [(c, count - 1 - c) for c in range(count)])]
  transfers between devices with their start and end apart: 8 -> 13, of which waited for: 4 -> 3; matrix products, arithmetic and copies ran while one was open for 20% -> 23% of each run, Pallas kernels for 47% -> 48%
where the time goes in v3:
time: 194 us
  Pallas kernels  93.7 us (48%)
  local copies, waits for them, and re-layouts  23.9 us (12%)
  waiting for transfers between devices  21.6 us (11%)
  matrix products  18.2 us (9%)
  between operations  14.1 us (7%)
  starting transfers between devices  12.4 us (6%)
  other arithmetic  9.61 us (5%)
    pallas_call x2, Pallas kernels, exchange(): pl.pallas_call(functools.partial(exchange_kernel, count, by_core), out_sh...  63.2 us
    unnamed x29, local copies, waits for them, and re-layouts  19 us
    dot_general x5, matrix products, dot(): lax.dot_general(left, right, dims, preferred_element_type=jnp.float32)  18.2 us
    pallas_call x1, Pallas kernels, backward_units(): pl.pallas_call(backward_kernel, grid_spec=pltpu.PrefetchScalarGridSpec(nu...  16.9 us
    pallas_call x1, Pallas kernels, forward_units(): pl.pallas_call(forward_kernel, grid_spec=pltpu.PrefetchScalarGridSpec(num...  12.4 us
    all_gather x2, waiting for transfers between devices, paired_device(): lax.all_gather(column_chunk(grad_out, own_tiles, chunk), 'head', axis=1,...  9.54 us
    ppermute x2, waiting for transfers between devices, swapped(): lax.ppermute(value, 'ctx', [(c, count - 1 - c) for c in range(count)])  7.79 us
    ppermute x6, starting transfers between devices, chip_parts(): lax.ppermute(part, 'ctx', [(c, c ^ 2 * turn) for c in range(count)])  7.04 us
  transfers between devices with their start and end apart: 13, of which 3 were waited for; matrix products, arithmetic and copies ran while one was open for 23% of the time, Pallas kernels for 48%

profile of v3, /device:TPU:0, one launch (start us, length us, event | category | flops | bytes accessed | tf_op | source)
XLA Modules:
  0.0 193.6 jit_solution(11807841365754170620)
XLA Ops:
  9.9 32.8 %shard_map.101 = (bf16[8,512,256]{2,1,0:T(8,128)(2,1)S(1)}, bf16[512,256]{1,0:T(8,128)(2,1)S(1)}) custom-call(bf16[2,512,256]{2,1,0:T(8,128)(2,1)S(1)} %maximum_maximum_fusion.blocks_ref, bf16[2,512,256]{2,1,0:T(8,128)(2,1)S(1)} %pad_maximum_fusion.1.halves_ref), custom_call_target="tpu_custom_call" | custom-call | bytes 2097152 | tf_op jit(solution)/shard_map/pallas_call | solution.py:278
  46.6 12.4 %shard_map.102 = (bf16[2,512,256]{2,1,0:T(8,128)(2,1)S(1)}, f32[2,2,512]{2,1,0:T(2,128)S(1)}) custom-call(s32[2,8]{1,0:T(2,128)S(1)} %broadcast_select_fusion.1.rows_ref, bf16[2,512,256]{2,1,0:T(8,128)(2,1)S(1)} %pad_maximum_fusion.2.q_ref, bf16[8,512,256]{2,1,0:T(8,128)(2,1)S(1)} %copy-done.2), custom_call_target="tpu_custom_call" | custom-call | flops 1342177280 | bytes 2097152 | tf_op jit(solution)/shard_map/pallas_call | solution.py:364
  59.0 3.3 %collective-permute-start = (bf16[512,256]{1,0:T(8,128)(2,1)S(1)}, bf16[512,256]{1,0:T(8,128)(2,1)S(1)}, u32[]{:S(2)}, u32[]{:S(2)}) collective-permute-start(bf16[512,256]{1,0:T(8,128)(2,1)S(1)} %slice_bitcast_fusion.8), channel_id=1, source_target_pairs={{0,28},{4,24},{8,20},{12,16},{16,12},{20,8},{24,4},{28,0},{1,29},{... | collective-permute-start | bytes 786440 | tf_op jit(solution)/shard_map/ppermute | solution.py:488
  63.4 1.9 slice_dynamic-update-slice_fusion.7
  65.3 1.9 slice_dynamic-update-slice_fusion.6
  67.2 1.9 slice_dynamic-update-slice_fusion.5
  69.1 1.9 slice_dynamic-update-slice_fusion.4
  71.0 2.0 %slice_dynamic-update-slice_fusion.3 = (bf16[512,2048]{1,0:T(8,128)(2,1)}, bf16[512,2048]{1,0:T(8,128)(2,1)}) fusion(bf16[512,2048]{1,0:T(8,128)(2,1)} %get-tuple-element.55, bf16[512,4096]{1,0:T(8,128)(2,1)} %param.9, bf16[512,2048]{1,0:T(8,128)(2,1)} %get-tuple-element.56), kind=kLoop, calls=%fused_computation.43 | loop fusion | bytes 1048576
  73.7 3.0 %convolution_convert_fusion.2 = bf16[2048,512]{1,0:T(8,128)(2,1)S(1)} fusion(bf16[512,2048]{1,0:T(8,128)(2,1)} %all-gather.5.cloned.1.call-done, bf16[512,256]{1,0:T(8,128)(2,1)} %get-tuple-element.82, bf16[512,256]{1,0:T(8,128)(2,1)S(1)} %get-tuple-element.81), kind=kOutput, calls=%fused_computation.4 | convolution fusion | flops 1075838976 | bytes 4718592 | tf_op jit(solution)/shard_map/dot_general | solution.py:234
  77.8 1.9 slice_dynamic-update-slice_fusion.2
  79.7 2.0 %slice_dynamic-update-slice_fusion.1 = (bf16[512,2048]{1,0:T(8,128)(2,1)}, bf16[512,2048]{1,0:T(8,128)(2,1)}) fusion(bf16[512,2048]{1,0:T(8,128)(2,1)} %get-tuple-element.51, bf16[512,4096]{1,0:T(8,128)(2,1)} %param.9, bf16[512,2048]{1,0:T(8,128)(2,1)} %get-tuple-element.52), kind=kLoop, calls=%fused_computation.41 | loop fusion | bytes 1048576
  81.7 1.9 slice_dynamic-update-slice_fusion
  83.6 6.6 %convolution_convert_fusion = bf16[512,4096]{1,0:T(8,128)(2,1)} fusion(bf16[512,4096]{1,0:T(8,128)(2,1)} %param.9, bf16[512,256]{1,0:T(8,128)(2,1)S(1)} %copy-done.8, bf16[512,256]{1,0:T(8,128)(2,1)S(1)} %get-tuple-element.81), kind=kOutput, calls=%fused_computation.1 | convolution fusion | flops 2150629376 | bytes 8912896 | tf_op jit(solution)/shard_map/dot_general | solution.py:234
  90.2 1.7 fusion.1
  93.6 2.6 %collective-permute-start.4 = (bf16[256,512]{1,0:T(8,128)(2,1)S(1)}, bf16[256,512]{1,0:T(8,128)(2,1)S(1)}, u32[]{:S(2)}, u32[]{:S(2)}) collective-permute-start(bf16[256,512]{1,0:T(8,128)(2,1)S(1)} %get-tuple-element.68), channel_id=1, source_target_pairs={{0,24},{4,28},{8,16},{12,20},{16,8},{20,12},{24,0},{28,4},{1,25},{... | collective-permute-start | bytes 786440 | tf_op jit(solution)/shard_map/ppermute | solution.py:503
  96.2 2.9 %fusion.7 = f32[512,512]{1,0:T(8,128)S(1)} fusion(bf16[512,2048]{1,0:T(8,128)(2,1)S(1)} %copy-done.9, bf16[512,2048]{1,0:T(8,128)(2,1)} %get-tuple-element.48), kind=kOutput, calls=%fused_computation.78 | convolution fusion | flops 1073741824 | bytes 5242880 | tf_op jit(solution)/shard_map/dot_general | solution.py:234
  99.1 9.5 %all-gather.3.cloned.1.call-done = bf16[512,2048]{1,0:T(8,128)(2,1)} async-done(((bf16[512,512]{1,0:T(8,128)(2,1)}), bf16[512,2048]{1,0:T(8,128)(2,1)}) %all-gather.3.cloned.1.call-update) | async-done | bytes 2097168 | tf_op jit(solution)/shard_map/all_gather | solution.py:541
  109.6 2.9 %convolution_convert_fusion.1 = bf16[2048,512]{1,0:T(8,128)(2,1)S(1)} fusion(bf16[512,2048]{1,0:T(8,128)(2,1)} %all-gather.3.cloned.1.call-done, bf16[512,256]{1,0:T(8,128)(2,1)} %get-tuple-element.82, bf16[512,256]{1,0:T(8,128)(2,1)S(1)} %copy-done.7), kind=kOutput, calls=%fused_computation.3 | convolution fusion | flops 1075838976 | bytes 4718592 | tf_op jit(solution)/shard_map/dot_general | solution.py:234
  114.1 2.9 %fusion.8 = f32[512,512]{1,0:T(8,128)S(1)} fusion(bf16[512,2048]{1,0:T(8,128)(2,1)S(1)} %copy-done.10, bf16[512,2048]{1,0:T(8,128)(2,1)} %get-tuple-element.47), kind=kOutput, calls=%fused_computation.79 | convolution fusion | flops 1073741824 | bytes 5242880 | tf_op jit(solution)/shard_map/dot_general | solution.py:234
  117.3 1.8 collective-permute-start.6
  119.0 7.8 %collective-permute-done.6 = bf16[512,256]{1,0:T(8,128)(2,1)S(1)} collective-permute-done((bf16[512,256]{1,0:T(8,128)(2,1)S(1)}, bf16[512,256]{1,0:T(8,128)(2,1)S(1)}, u32[]{:S(2)}, u32[]{:S(2)}) %collective-permute-start.6) | collective-permute-done | bytes 262176 | tf_op jit(solution)/shard_map/ppermute | solution.py:488
  131.0 16.9 %shard_map.103 = (bf16[2,512,256]{2,1,0:T(8,128)(2,1)S(1)}, bf16[8,512,256]{2,1,0:T(8,128)(2,1)S(1)}) custom-call(s32[2,8]{1,0:T(2,128)S(1)} %broadcast_select_fusion.1.rows_ref, bf16[2,512,256]{2,1,0:T(8,128)(2,1)S(1)} %pad_maximum_fusion.2.q_ref, bf16[2,512,256]{2,1,0:T(8,128)(2,1)S(1)} %pad_maximum_fusion.5.g_ref, ...), custom_call_target="tpu_custom_call" | custom-call | flops 3355443200 | bytes 4194304 | tf_op jit(solution)/shard_map/pallas_call | solution.py:456
  147.9 30.4 %shard_map.104 = (bf16[8,512,256]{2,1,0:T(8,128)(2,1)S(1)}, bf16[512,256]{1,0:T(8,128)(2,1)S(1)}) custom-call(bf16[8,512,256]{2,1,0:T(8,128)(2,1)S(1)} %get-tuple-element.38.blocks_ref, bf16[2,512,256]{2,1,0:T(8,128)(2,1)S(1)} %get-tuple-element.37.halves_ref), custom_call_target="tpu_custom_call" | custom-call | bytes 5242880 | tf_op jit(solution)/shard_map/pallas_call | solution.py:278
  182.8 4.2 %reduce-scatter.2.cloned.1.call-done = bf16[512,1024]{1,0:T(8,128)(2,1)} async-done(((bf16[512,4096]{1,0:T(8,128)(2,1)}), bf16[512,1024]{1,0:T(8,128)(2,1)}) %reduce-scatter.2.cloned.1.call-update) | async-done | bytes 1048592 | tf_op jit(solution)/shard_map/reduce_scatter | solution.py:574
  (75 shorter events, 22.7 us)
Async XLA Ops:
  7.2 37.1 %copy-start = (s32[8,8]{1,0:T(8,128)S(1)}, s32[8,8]{1,0:T(8,128)}, u32[]{:S(2)}) copy-start(s32[8,8]{1,0:T(8,128)} %param.10) | copy-start | bytes 772
  7.2 2.3 %copy-start.3 = (bf16[512,512]{1,0:T(8,128)(2,1)S(1)}, bf16[512,512]{1,0:T(8,128)(2,1)}, u32[]{:S(2)}) copy-start(bf16[512,512]{1,0:T(8,128)(2,1)} %param.6) | copy-start | bytes 1572868
  7.2 66.5 %all-gather.5.cloned.1.call-start = ((), (), s32[]{:S(2)}) async-start(), calls=%async_computation.2 | async-start | bytes 2621440 | tf_op jit(solution)/shard_map/all_gather | solution.py:541
  8.6 1.1 copy-start.4
  8.6 1.2 copy-start.5
  9.4 99.2 %all-gather.3.cloned.1.call-start = ((), (), s32[]{:S(2)}) async-start(), calls=%async_computation.1 | async-start | bytes 2621440 | tf_op jit(solution)/shard_map/all_gather | solution.py:541
  42.8 1.4 copy-start.1
  45.0 1.6 copy-start.2
  59.0 14.0 %collective-permute-start = (bf16[512,256]{1,0:T(8,128)(2,1)S(1)}, bf16[512,256]{1,0:T(8,128)(2,1)S(1)}, u32[]{:S(2)}, u32[]{:S(2)}) collective-permute-start(bf16[512,256]{1,0:T(8,128)(2,1)S(1)} %slice_bitcast_fusion.8), channel_id=1, source_target_pairs={{0,28},{4,24},{8,20},{12,16},{16,12},{20,8},{24,4},{28,0},{1,29},{... | collective-permute-start | bytes 786440 | tf_op jit(solution)/shard_map/ppermute | solution.py:488
  63.1 123.9 %reduce-scatter.2.cloned.1.call-start = ((), (), s32[]{:S(2)}) async-start(), calls=%async_computation.3 | async-start | bytes 5242880 | tf_op jit(solution)/shard_map/reduce_scatter | solution.py:574
  73.7 9.9 %copy-start.6 = (bf16[512,256]{1,0:T(8,128)(2,1)}, bf16[512,256]{1,0:T(8,128)(2,1)S(1)}, u32[]{:S(2)}) copy-start(bf16[512,256]{1,0:T(8,128)(2,1)S(1)} %get-tuple-element.81) | copy-start | bytes 786436
  77.8 12.4 %collective-permute-start.1 = (bf16[4,256,512]{2,1,0:T(8,128)(2,1)}, bf16[4,256,512]{2,1,0:T(8,128)(2,1)}, u32[]{:S(2)}, u32[]{:S(2)}) collective-permute-start(bf16[4,256,512]{2,1,0:T(8,128)(2,1)} %select_bitcast_fusion.1), channel_id=1, source_target_pairs={{0,4},{4,0},{8,12},{12,8},{16,20},{20,16},{24,28},{28,24},{1,5},{5... | collective-permute-start | bytes 3145736 | tf_op jit(solution)/shard_map/ppermute | solution.py:495
  79.7 3.9 %copy-start.8 = (bf16[512,256]{1,0:T(8,128)(2,1)S(1)}, bf16[512,256]{1,0:T(8,128)(2,1)}, u32[]{:S(2)}) copy-start(bf16[512,256]{1,0:T(8,128)(2,1)} %get-tuple-element.82) | copy-start | bytes 786436
  91.8 4.4 %copy-start.9 = (bf16[512,2048]{1,0:T(8,128)(2,1)S(1)}, bf16[512,2048]{1,0:T(8,128)(2,1)}, u32[]{:S(2)}) copy-start(bf16[512,2048]{1,0:T(8,128)(2,1)} %all-gather.5.cloned.1.call-done) | copy-start | bytes 6291460
  92.7 15.9 %collective-permute-start.2 = (bf16[256,512]{1,0:T(8,128)(2,1)}, bf16[256,512]{1,0:T(8,128)(2,1)S(1)}, u32[]{:S(2)}, u32[]{:S(2)}) collective-permute-start(bf16[256,512]{1,0:T(8,128)(2,1)} %get-tuple-element.70), channel_id=1, source_target_pairs={{0,8},{4,12},{8,0},{12,4},{16,24},{20,28},{24,16},{28,20},{1,9},{5... | collective-permute-start | bytes 786440 | tf_op jit(solution)/shard_map/ppermute | solution.py:503
  92.7 15.9 %collective-permute-start.3 = (bf16[256,512]{1,0:T(8,128)(2,1)}, bf16[256,512]{1,0:T(8,128)(2,1)S(1)}, u32[]{:S(2)}, u32[]{:S(2)}) collective-permute-start(bf16[256,512]{1,0:T(8,128)(2,1)} %get-tuple-element.69), channel_id=1, source_target_pairs={{0,16},{4,20},{8,24},{12,28},{16,0},{20,4},{24,8},{28,12},{1,17},{... | collective-permute-start | bytes 786440 | tf_op jit(solution)/shard_map/ppermute | solution.py:503
  93.6 15.1 %collective-permute-start.4 = (bf16[256,512]{1,0:T(8,128)(2,1)S(1)}, bf16[256,512]{1,0:T(8,128)(2,1)S(1)}, u32[]{:S(2)}, u32[]{:S(2)}) collective-permute-start(bf16[256,512]{1,0:T(8,128)(2,1)S(1)} %get-tuple-element.68), channel_id=1, source_target_pairs={{0,24},{4,28},{8,16},{12,20},{16,8},{20,12},{24,0},{28,4},{1,25},{... | collective-permute-start | bytes 786440 | tf_op jit(solution)/shard_map/ppermute | solution.py:503
  108.7 1.0 copy-start.7
  112.5 1.6 copy-start.10
  112.6 14.3 %collective-permute-start.5 = (bf16[4,256,512]{2,1,0:T(8,128)(2,1)S(1)}, bf16[4,256,512]{2,1,0:T(8,128)(2,1)S(1)}, u32[]{:S(2)}, u32[]{:S(2)}) collective-permute-start(bf16[4,256,512]{2,1,0:T(8,128)(2,1)S(1)} %select_bitcast_fusion), channel_id=1, source_target_pairs={{0,4},{4,0},{8,12},{12,8},{16,20},{20,16},{24,28},{28,24},{1,5},{5... | collective-permute-start | bytes 3145736 | tf_op jit(solution)/shard_map/ppermute | solution.py:495
  117.3 9.5 %collective-permute-start.6 = (bf16[512,256]{1,0:T(8,128)(2,1)S(1)}, bf16[512,256]{1,0:T(8,128)(2,1)S(1)}, u32[]{:S(2)}, u32[]{:S(2)}) collective-permute-start(bf16[512,256]{1,0:T(8,128)(2,1)S(1)} %get-tuple-element.84), channel_id=1, source_target_pairs={{0,28},{4,24},{8,20},{12,16},{16,12},{20,8},{24,4},{28,0},{1,29},{... | collective-permute-start | bytes 786440 | tf_op jit(solution)/shard_map/ppermute | solution.py:488
  127.4 20.4 %collective-permute-start.7 = (bf16[256,512]{1,0:T(8,128)(2,1)S(1)}, bf16[256,512]{1,0:T(8,128)(2,1)S(1)}, u32[]{:S(2)}, u32[]{:S(2)}) collective-permute-start(bf16[256,512]{1,0:T(8,128)(2,1)S(1)} %get-tuple-element.66), channel_id=1, source_target_pairs={{0,8},{4,12},{8,0},{12,4},{16,24},{20,28},{24,16},{28,20},{1,9},{5... | collective-permute-start | bytes 786440 | tf_op jit(solution)/shard_map/ppermute | solution.py:503
  129.0 18.9 %collective-permute-start.8 = (bf16[256,512]{1,0:T(8,128)(2,1)S(1)}, bf16[256,512]{1,0:T(8,128)(2,1)S(1)}, u32[]{:S(2)}, u32[]{:S(2)}) collective-permute-start(bf16[256,512]{1,0:T(8,128)(2,1)S(1)} %get-tuple-element.65), channel_id=1, source_target_pairs={{0,16},{4,20},{8,24},{12,28},{16,0},{20,4},{24,8},{28,12},{1,17},{... | collective-permute-start | bytes 786440 | tf_op jit(solution)/shard_map/ppermute | solution.py:503
  130.3 17.5 %collective-permute-start.9 = (bf16[256,512]{1,0:T(8,128)(2,1)S(1)}, bf16[256,512]{1,0:T(8,128)(2,1)S(1)}, u32[]{:S(2)}, u32[]{:S(2)}) collective-permute-start(bf16[256,512]{1,0:T(8,128)(2,1)S(1)} %get-tuple-element.64), channel_id=1, source_target_pairs={{0,24},{4,28},{8,16},{12,20},{16,8},{20,12},{24,0},{28,4},{1,25},{... | collective-permute-start | bytes 786440 | tf_op jit(solution)/shard_map/ppermute | solution.py:503
Sparse Core Ops, SparseCore 0:
  10.2 48.6 all-gather.4
  63.2 45.3 all-gather.2
  111.5 75.4 reduce-scatter.1

commit v4 on v3

--- a/solution.py
+++ b/solution.py
@@ -234,68 +234,175 @@
     return lax.dot_general(left, right, dims, preferred_element_type=jnp.float32)
 
 
-def greet(peers, count):
-    barrier = pltpu.get_barrier_semaphore()
-    for peer in peers:
-        pl.semaphore_signal(barrier, inc=1, device_id={"ctx": peer}, device_id_type=MESH)
-    pl.semaphore_wait(barrier, count)
-
-
-def remote(source, target, send_sem, recv_sem, peer):
+def remote(source, target, send_sem, recv_sem, axis, peer):
     return pltpu.make_async_remote_copy(
         src_ref=source,
         dst_ref=target,
         send_sem=send_sem,
         recv_sem=recv_sem,
-        device_id={"ctx": peer},
+        device_id={axis: peer},
         device_id_type=MESH,
     )
 
 
-def exchange_kernel(count, by_core, blocks_ref, halves_ref, blocks_all, other, send, recv, half, local):
-    me = lax.axis_index("ctx")
+def exchange_kernel(
+    count,
+    groups,
+    spread,
+    blocks_ref,
+    halves_ref,
+    columns_ref,
+    blocks_all,
+    other,
+    columns_all,
+    send,
+    recv,
+    half,
+    group_send,
+    group_recv,
+    local,
+):
+    me, group = lax.axis_index("ctx"), lax.axis_index("head")
     core = lax.rem(me, 2)
-    greet([lax.rem(me + step, count) for step in range(1, count)], count - 1)
-    source = halves_ref.at[1 - core] if by_core else halves_ref.at[1]
-    copies = [remote(source, other, half.at[0], half.at[1], count - 1 - me)]
-    copies[0].start()
+    width = columns_all.shape[1] // groups
+
+    def columns_of(ref, index):
+        return ref.at[:, pl.ds(pl.multiple_of(index * width, width), width)]
+
+    barrier = pltpu.get_barrier_semaphore()
+    for axis, rank, size in (("ctx", me, count), ("head", group, groups)):
+        for step in range(1, size):
+            pl.semaphore_signal(
+                barrier,
+                inc=1,
+                device_id={axis: lax.rem(rank + step, size)},
+                device_id_type=MESH,
+            )
+    pl.semaphore_wait(barrier, count + groups - 2)
+
+    copies = []
+    source = halves_ref.at[1 - core] if spread else halves_ref.at[1]
+    copies.append(remote(source, other, half.at[0], half.at[1], "ctx", count - 1 - me))
+    for step in range(1, groups):
+        peer = lax.rem(group + step, groups)
+        copies.append(
+            remote(
+                columns_ref if spread else columns_of(columns_ref, peer),
+                columns_of(columns_all, group),
+                group_send.at[step],
+                group_recv.at[step],
+                "head",
+                peer,
+            )
+        )
     for step in range(1, count):
         peer = lax.rem(me + step, count)
-        index = lax.rem(peer, 2) if by_core else peer
-        copy = remote(blocks_ref.at[index], blocks_all.at[me], send.at[step], recv.at[step], peer)
+        index = lax.rem(peer, 2) if spread else peer
+        copies.append(
+            remote(
+                blocks_ref.at[index],
+                blocks_all.at[me],
+                send.at[step],
+                recv.at[step],
+                "ctx",
+                peer,
+            )
+        )
+    for copy in copies:
         copy.start()
-        copies.append(copy)
-    index = core if by_core else me
-    mine = pltpu.make_async_copy(blocks_ref.at[index], blocks_all.at[me], local)
-    mine.start()
-    mine.wait()
-    for copy in copies:
+    own = [
+        pltpu.make_async_copy(blocks_ref.at[core if spread else me], blocks_all.at[me], local.at[0]),
+        pltpu.make_async_copy(
+            columns_ref if spread else columns_of(columns_ref, group),
+            columns_of(columns_all, group),
+            local.at[1],
+        ),
+    ]
+    for copy in own:
+        copy.start()
+    for copy in own + copies:
         copy.wait()
 
 
-def exchange(by_core, collective_id, count, blocks, units):
+def exchange(spread, collective_id, count, groups, blocks, units, columns):
     any_space = pl.BlockSpec(memory_space=pl.ANY)
+    width = columns.shape[1] * (groups if spread else 1)
     return pl.pallas_call(
-        functools.partial(exchange_kernel, count, by_core),
+        functools.partial(exchange_kernel, count, groups, spread),
         out_shape=(
             jax.ShapeDtypeStruct((count,) + blocks.shape[1:], blocks.dtype),
             jax.ShapeDtypeStruct(units.shape[1:], units.dtype),
-        ),
-        in_specs=[any_space, any_space],
-        out_specs=(any_space, any_space),
+            jax.ShapeDtypeStruct((columns.shape[0], width), columns.dtype),
+        ),
+        in_specs=[any_space] * 3,
+        out_specs=(any_space,) * 3,
         scratch_shapes=[
             pltpu.SemaphoreType.DMA((count,)),
             pltpu.SemaphoreType.DMA((count,)),
             pltpu.SemaphoreType.DMA((2,)),
-            pltpu.SemaphoreType.DMA,
+            pltpu.SemaphoreType.DMA((groups,)),
+            pltpu.SemaphoreType.DMA((groups,)),
+            pltpu.SemaphoreType.DMA((2,)),
         ],
         compiler_params=pltpu.CompilerParams(
             collective_id=collective_id, has_side_effects=True, vmem_limit_bytes=VMEM_BYTES
         ),
         cost_estimate=pl.CostEstimate(
-            flops=0, bytes_accessed=2 * blocks.size * 2 + units.size * 4, transcendentals=0
-        ),
-    )(blocks, units)
+            flops=0, bytes_accessed=4 * blocks.size * 2 + units.size * 4, transcendentals=0
+        ),
+    )(blocks, units, columns)
+
+
+def grad_attn_kernel(tiles, *refs):
+    pieces, w_ref, out_ref = refs[:-2], refs[-2], refs[-1]
+    width = w_ref.shape[1] // tiles // len(pieces)
+    total = jnp.zeros(out_ref.shape, jnp.float32)
+    for tile in range(tiles):
+        for chunk, piece in enumerate(pieces):
+            start = (tile * len(pieces) + chunk) * width
+            total += dot(
+                piece[:, tile * width : (tile + 1) * width],
+                w_ref[:, start : start + width],
+                CONTRACT_LAST,
+            )
+    out_ref[...] = total.astype(out_ref.dtype)
+
+
+def grad_attn_of(pieces, w_out, tiles):
+    tokens = pieces[0].shape[0]
+    return pl.pallas_call(
+        functools.partial(grad_attn_kernel, tiles),
+        out_shape=jax.ShapeDtypeStruct((tokens, w_out.shape[0]), jnp.bfloat16),
+        compiler_params=pltpu.CompilerParams(vmem_limit_bytes=VMEM_BYTES),
+        cost_estimate=pl.CostEstimate(
+            flops=2 * tokens * w_out.size, bytes_accessed=4 * w_out.size, transcendentals=0
+        ),
+    )(*pieces, w_out)
+
+
+def out_terms_kernel(groups, attn_ref, w_ref, *out_refs):
+    for group in range(groups):
+        start = group * (w_ref.shape[1] // groups)
+        for out_ref in out_refs:
+            width = out_ref.shape[1] // groups
+            out_ref[:, group * width : (group + 1) * width] = dot(
+                attn_ref[...], w_ref[:, start : start + width]
+            ).astype(out_ref.dtype)
+            start += width
+
+
+def out_terms_of(attn, w_out, groups, widths):
+    tokens = attn.shape[0]
+    return pl.pallas_call(
+        functools.partial(out_terms_kernel, groups),
+        out_shape=tuple(
+            jax.ShapeDtypeStruct((tokens, groups * width), jnp.bfloat16) for width in widths
+        ),
+        compiler_params=pltpu.CompilerParams(vmem_limit_bytes=VMEM_BYTES),
+        cost_estimate=pl.CostEstimate(
+            flops=2 * tokens * w_out.size, bytes_accessed=4 * w_out.size, transcendentals=0
+        ),
+    )(attn, w_out)
 
 
 def head_part(value, head):
@@ -537,10 +644,8 @@
     core, chip = lax.rem(me, 2), lax.div(me, 2)
     tokens = query_proj.shape[0]
     own_tiles = count // groups
-    pieces = [
-        lax.all_gather(column_chunk(grad_out, own_tiles, chunk), "head", axis=1, tiled=True)
-        for chunk in range(2)
-    ]
+    chunks = [column_chunk(grad_out, own_tiles, chunk) for chunk in range(2)]
+    last_piece = lax.all_gather(chunks[1], "head", axis=1, tiled=True)
     key_halves, value_halves = halves_of(projected_keys), halves_of(projected_values)
 
     def own_half(halves):
@@ -556,32 +661,50 @@
         return merged_cores(terms, core, count)
 
     query_halves = halves_of(query_proj)
-    kv_all, q_other = exchange(
-        True, 0, count, jnp.concatenate([key_halves, value_halves], 2), query_halves
-    )
-    weights = [column_chunk(w_out, count, chunk) for chunk in range(2)]
+    kv_all, q_other, first_piece = exchange(
+        True,
+        0,
+        count,
+        groups,
+        jnp.concatenate([key_halves, value_halves], 2),
+        query_halves,
+        chunks[0],
+    )
     q_units = jnp.stack([own_half(query_halves), q_other])
     rows = jnp.take(attended_blocks, jnp.stack([me, count - 1 - me]), axis=0)
     attn_units, totals = forward_units(rows, q_units, kv_all)
     attn = both_halves(attn_units[0], swapped(attn_units[1], count))
-    out_terms = dot(attn, w_out).astype(jnp.bfloat16)
-    first_merged = weight_terms(pieces[0], attn)
-    first_grad = dot(pieces[0], weights[0], CONTRACT_LAST)
-    first_parts = chip_parts(first_merged, chip, count)
-    last_piece, out_terms, first_parts, first_grad = lax.optimization_barrier(
-        (pieces[1], out_terms, first_parts, first_grad)
-    )
-    layer_out = lax.psum_scatter(out_terms, "head", scatter_dimension=1, tiled=True)
-    grad_attn = first_grad + dot(last_piece, weights[1], CONTRACT_LAST)
-    grad_halves = halves_of(grad_attn.astype(jnp.bfloat16))
+    own_columns = grad_out.shape[1]
+    direct = own_columns // 4
+    scattered_terms, direct_terms = out_terms_of(
+        attn, w_out, groups, (own_columns - direct, direct)
+    )
+    scattered = lax.psum_scatter(scattered_terms, "head", scatter_dimension=1, tiled=True)
+    grad_attn = grad_attn_of([first_piece, last_piece], w_out, count)
+    grad_halves = halves_of(grad_attn)
     grad_other = swapped(own_half(grad_halves[::-1]), count)
     g_units = jnp.stack([own_half(grad_halves), grad_other])
+    first_piece, last_piece, direct_terms = lax.optimization_barrier(
+        (first_piece, last_piece, direct_terms)
+    )
+    first_merged = weight_terms(first_piece, attn)
     last_merged = weight_terms(last_piece, attn)
-    last_merged, g_units = lax.optimization_barrier((last_merged, g_units))
+    first_merged, last_merged, g_units = lax.optimization_barrier(
+        (first_merged, last_merged, g_units)
+    )
+    first_parts = chip_parts(first_merged, chip, count)
     last_parts = chip_parts(last_merged, chip, count)
     dq_units, dkv = backward_units(rows, q_units, g_units, attn_units, totals, kv_all)
-    last_parts, dq_units, dkv = lax.optimization_barrier((last_parts, dq_units, dkv))
-    dkv_all, dq_other = exchange(False, 1, count, dkv, dq_units)
+    first_parts, last_parts, dq_units, dkv = lax.optimization_barrier(
+        (first_parts, last_parts, dq_units, dkv)
+    )
+    dkv_all, dq_other, direct_all = exchange(
+        False, 1, count, groups, dkv, dq_units, direct_terms
+    )
+    direct_out = direct_all[:, :direct].astype(jnp.float32)
+    for index in range(1, groups):
+        direct_out += direct_all[:, index * direct : (index + 1) * direct].astype(jnp.float32)
+    layer_out = jnp.concatenate([scattered, direct_out.astype(jnp.bfloat16)], 1)
 
     def kept(merged):
         return lax.dynamic_index_in_dim(merged, chip, 0, keepdims=False)

time: 194 us -> 225 us (1.16); the launches traced: 194 us -> 221 us
  Pallas kernels: 93.7 us -> 154 us
  local copies, waits for them, and re-layouts: 23.9 us -> 5.74 us
  matrix products: 18.2 us -> 4.17 us
  other arithmetic: 9.61 us -> 14.3 us
  waiting for transfers between devices: 21.6 us -> 18.4 us
  starting transfers between devices: 12.4 us -> 9.42 us
    pallas_call x2 -> x4, Pallas kernels: 63.2 us -> 124 us  [the longest x2 113 us: exchange(): pl.pallas_call(functools.partial(exchange_kernel, count, groups, spread),...]
    unnamed x29 -> x34, local copies, waits for them, and re-layouts: 19 us -> 3.54 us
    dot_general x5 -> x2, matrix products: 18.2 us -> 4.17 us  [dot(): lax.dot_general(left, right, dims, preferred_element_type=jnp.float32)]
    all_gather x2 -> x1, waiting for transfers between devices: 9.54 us -> 0.02 us  [paired_device(): last_piece = lax.all_gather(chunks[1], 'head', axis=1, tiled=True)]
    ppermute x2, waiting for transfers between devices: 7.79 us -> 14.3 us  [swapped(): lax.ppermute(value, 'ctx', [(c, count - 1 - c) for c in range(count)])]
    reduce_scatter x1, waiting for transfers between devices: 4.22 us -> 0.02 us  [paired_device(): lax.psum_scatter(scattered_terms, 'head', scatter_dimension=1, tiled=True)]
    ppermute x6, waiting for transfers between devices: 0.02 us -> 3.98 us  [chip_parts(): lax.ppermute(part, 'ctx', [(c, c ^ 2 * turn) for c in range(count)])]
    ppermute x2, starting transfers between devices: 5.01 us -> 2 us  [swapped(): lax.ppermute(value, 'ctx', [(c, count - 1 - c) for c in range(count)])]
  transfers between devices with their start and end apart: 13 -> 12, of which waited for: 3 -> 3; matrix products, arithmetic and copies ran while one was open for 23% -> 7% of each run, Pallas kernels for 48% -> 70%
where the time goes in v4:
time: 225 us; the launch traced here: 221 us
  Pallas kernels  154 us (68%)
  waiting for transfers between devices  18.4 us (8%)
  between operations  14.4 us (6%)
  other arithmetic  14.3 us (6%)
  starting transfers between devices  9.42 us (4%)
  local copies, waits for them, and re-layouts  5.74 us (3%)
  matrix products  4.17 us (2%)
    pallas_call x2, Pallas kernels, exchange(): pl.pallas_call(functools.partial(exchange_kernel, count, groups, spread),...  113 us
    pallas_call x1, Pallas kernels, backward_units(): pl.pallas_call(backward_kernel, grid_spec=pltpu.PrefetchScalarGridSpec(nu...  16.9 us
    ppermute x2, waiting for transfers between devices, swapped(): lax.ppermute(value, 'ctx', [(c, count - 1 - c) for c in range(count)])  14.3 us
    pallas_call x1, Pallas kernels, forward_units(): pl.pallas_call(forward_kernel, grid_spec=pltpu.PrefetchScalarGridSpec(num...  12.4 us
    ppermute x6, starting transfers between devices, chip_parts(): lax.ppermute(part, 'ctx', [(c, c ^ 2 * turn) for c in range(count)])  6.88 us
    pallas_call x1, Pallas kernels, out_terms_of(): pl.pallas_call(functools.partial(out_terms_kernel, groups), out_shape=tup...  6.22 us
    pallas_call x1, Pallas kernels, grad_attn_of(): pl.pallas_call(functools.partial(grad_attn_kernel, tiles), out_shape=jax....  4.55 us
  transfers between devices with their start and end apart: 12, of which 3 were waited for; matrix products, arithmetic and copies ran while one was open for 7% of the time, Pallas kernels for 70%

profile of v4, /device:TPU:0, one launch (start us, length us, event | category | flops | bytes accessed | tf_op | source)
XLA Modules:
  0.0 220.8 jit_solution(15494246776252544735)
XLA Ops:
  7.2 1.3 fusion.3
  10.6 66.7 %shard_map.101 = (bf16[8,512,256]{2,1,0:T(8,128)(2,1)S(1)}, bf16[512,256]{1,0:T(8,128)(2,1)S(1)}, bf16[512,2048]{1,0:T(8,128)(2,1)S(1)}) custom-call(bf16[2,512,256]{2,1,0:T(8,128)(2,1)S(1)} %maximum_maximum_fusion.blocks_ref, bf16[2,512,256]{2,1,0:T(8,128)(2,1)S(1)} %pad_maximum_fusion.1.halves_ref, bf16[512,512]{1,0:T(8,128)(2,1)S(1)} %pad_maximum_fusion.2.columns_ref), custom_call_target="tpu_custom_call" | custom-call | bytes 3145728 | tf_op jit(solution)/shard_map/pallas_call | solution.py:330
  77.6 12.4 %shard_map.102 = (bf16[2,512,256]{2,1,0:T(8,128)(2,1)S(1)}, f32[2,2,512]{2,1,0:T(2,128)S(1)}) custom-call(s32[2,8]{1,0:T(2,128)S(1)} %broadcast_select_fusion.1.rows_ref, bf16[2,512,256]{2,1,0:T(8,128)(2,1)S(1)} %pad_maximum_fusion.3.q_ref, bf16[8,512,256]{2,1,0:T(8,128)(2,1)S(1)} %get-tuple-element.32.kv_ref), custom_call_target="tpu_custom_call" | custom-call | flops 1342177280 | bytes 2097152 | tf_op jit(solution)/shard_map/pallas_call | solution.py:471
  90.3 6.8 %collective-permute-done = bf16[512,256]{1,0:T(8,128)(2,1)S(1)} collective-permute-done((bf16[512,256]{1,0:T(8,128)(2,1)S(1)}, bf16[512,256]{1,0:T(8,128)(2,1)S(1)}, u32[]{:S(2)}, u32[]{:S(2)}) %collective-permute-start) | collective-permute-done | bytes 262176 | tf_op jit(solution)/shard_map/ppermute | solution.py:595
  97.9 6.2 %shard_map.103 = (bf16[512,3072]{1,0:T(8,128)(2,1)}, bf16[512,1024]{1,0:T(8,128)(2,1)S(1)}) custom-call(bf16[512,512]{1,0:T(8,128)(2,1)S(1)} %pad_maximum_fusion.4.attn_ref, bf16[512,4096]{1,0:T(8,128)(2,1)} %refs_2_.1), custom_call_target="tpu_custom_call" | custom-call | flops 2147483648 | bytes 8388608 | tf_op jit(solution)/shard_map/pallas_call | solution.py:396
  104.2 2.9 %convolution_convert_fusion = bf16[2048,512]{1,0:T(8,128)(2,1)S(1)} fusion(bf16[512,2048]{1,0:T(8,128)(2,1)} %all-gather.2.cloned.1.call-done.refs_1_, bf16[512,256]{1,0:T(8,128)(2,1)} %copy-done.12, bf16[512,256]{1,0:T(8,128)(2,1)S(1)} %get-tuple-element.75), kind=kOutput, calls=%fused_computation.2 | convolution fusion | flops 1075838976 | bytes 4718592 | tf_op jit(solution)/shard_map/dot_general | solution.py:234
  107.1 1.1 select_bitcast_fusion
  108.2 1.3 convolution_convert_fusion.1
  109.5 1.1 select_bitcast_fusion.1
  111.1 1.2 copy-done.1
  112.3 4.6 %shard_map.104 = bf16[512,512]{1,0:T(8,128)(2,1)S(1)} custom-call(bf16[512,2048]{1,0:T(8,128)(2,1)S(1)} %get-tuple-element.37.refs_0_, bf16[512,2048]{1,0:T(8,128)(2,1)S(1)} %copy-done.1, bf16[512,4096]{1,0:T(8,128)(2,1)} %refs_2_.1), custom_call_target="tpu_custom_call" | custom-call | flops 2147483648 | bytes 8388608 | tf_op jit(solution)/shard_map/pallas_call | solution.py:373
  117.6 1.8 collective-permute-start.3
  119.3 7.5 %collective-permute-done.3 = bf16[512,256]{1,0:T(8,128)(2,1)} collective-permute-done((bf16[512,256]{1,0:T(8,128)(2,1)}, bf16[512,256]{1,0:T(8,128)(2,1)}, u32[]{:S(2)}, u32[]{:S(2)}) %collective-permute-start.3) | collective-permute-done | bytes 262176 | tf_op jit(solution)/shard_map/ppermute | solution.py:595
  127.9 1.7 fusion
  129.8 1.7 fusion.1
  131.6 2.6 %collective-permute-start.6 = (bf16[256,512]{1,0:T(8,128)(2,1)S(1)}, bf16[256,512]{1,0:T(8,128)(2,1)S(1)}, u32[]{:S(2)}, u32[]{:S(2)}) collective-permute-start(bf16[256,512]{1,0:T(8,128)(2,1)S(1)} %get-tuple-element.62), channel_id=1, source_target_pairs={{0,24},{4,28},{8,16},{12,20},{16,8},{20,12},{24,0},{28,4},{1,25},{... | collective-permute-start | bytes 786440 | tf_op jit(solution)/shard_map/ppermute | solution.py:610
  135.3 2.5 %collective-permute-start.9 = (bf16[256,512]{1,0:T(8,128)(2,1)S(1)}, bf16[256,512]{1,0:T(8,128)(2,1)S(1)}, u32[]{:S(2)}, u32[]{:S(2)}) collective-permute-start(bf16[256,512]{1,0:T(8,128)(2,1)S(1)} %get-tuple-element.58), channel_id=1, source_target_pairs={{0,24},{4,28},{8,16},{12,20},{16,8},{20,12},{24,0},{28,4},{1,25},{... | collective-permute-start | bytes 786440 | tf_op jit(solution)/shard_map/ppermute | solution.py:610
  137.8 4.0 %collective-permute-done.6.refs_3_ = bf16[256,512]{1,0:T(8,128)(2,1)S(1)} collective-permute-done((bf16[256,512]{1,0:T(8,128)(2,1)S(1)}, bf16[256,512]{1,0:T(8,128)(2,1)S(1)}, u32[]{:S(2)}, u32[]{:S(2)}) %collective-permute-start.6) | collective-permute-done | bytes 262176 | tf_op jit(solution)/shard_map/ppermute | solution.py:610
  142.5 16.9 %shard_map.105 = (bf16[2,512,256]{2,1,0:T(8,128)(2,1)S(1)}, bf16[8,512,256]{2,1,0:T(8,128)(2,1)S(1)}) custom-call(s32[2,8]{1,0:T(2,128)S(1)} %broadcast_select_fusion.1.rows_ref, bf16[2,512,256]{2,1,0:T(8,128)(2,1)S(1)} %copy-done.4, bf16[2,512,256]{2,1,0:T(8,128)(2,1)S(1)} %pad_maximum_fusion.6.g_ref, bf16[2,512,256]{2,1,0:T(8,128)(2,1)S(1)} %copy-done.6, ...), custom_call_target="tpu_custom_call" | custom-call | flops 3355443200 | bytes 4194304 | tf_op jit(solution)/shard_map/pallas_call | solution.py:563
  159.5 1.3 copy-done.2
  160.8 46.2 %shard_map.106 = (bf16[8,512,256]{2,1,0:T(8,128)(2,1)S(1)}, bf16[512,256]{1,0:T(8,128)(2,1)S(1)}, bf16[512,1024]{1,0:T(8,128)(2,1)S(1)}) custom-call(bf16[8,512,256]{2,1,0:T(8,128)(2,1)} %copy-done.2, bf16[2,512,256]{2,1,0:T(8,128)(2,1)S(1)} %get-tuple-element.46.halves_ref, bf16[512,1024]{1,0:T(8,128)(2,1)S(1)} %get-tuple-element.47.columns_ref), custom_call_target="tpu_custom_call" | custom-call | bytes 9437184 | tf_op jit(solution)/shard_map/pallas_call | solution.py:330
  207.0 1.3 shard_map.107
  210.5 1.1 maximum_convert_fusion
  211.7 2.2 %pad_maximum_fusion = bf16[512,1024]{1,0:T(8,128)(2,1)} fusion(bf16[512,256]{1,0:T(8,128)(2,1)S(1)} %add_convert_fusion, bf16[512,768]{1,0:T(8,128)(2,1)} %reduce-scatter.2.cloned.1.call-done), kind=kLoop, calls=%fused_computation.12 | loop fusion | flops 2097152 | bytes 2097152 | tf_op jit(solution)/shard_map/concatenate | solution.py:707
  (77 shorter events, 9.9 us)
Async XLA Ops:
  7.2 2.4 %copy-start = (s32[8,8]{1,0:T(8,128)S(1)}, s32[8,8]{1,0:T(8,128)}, u32[]{:S(2)}) copy-start(s32[8,8]{1,0:T(8,128)} %param.10) | copy-start | bytes 772
  7.2 3.0 %copy-start.14 = (bf16[512,512]{1,0:T(8,128)(2,1)S(1)}, bf16[512,512]{1,0:T(8,128)(2,1)}, u32[]{:S(2)}) copy-start(bf16[512,512]{1,0:T(8,128)(2,1)} %param.6) | copy-start | bytes 1572868
  7.2 97.0 %all-gather.2.cloned.1.call-start = ((), (), s32[]{:S(2)}) async-start(), calls=%async_computation.2 | async-start | bytes 2621440 | tf_op jit(solution)/shard_map/all_gather | solution.py:648
  9.4 202.3 %reduce-scatter.2.cloned.1.call-start = ((), (), s32[]{:S(2)}) async-start(), calls=%async_computation.1 | async-start | bytes 3932160 | tf_op jit(solution)/shard_map/reduce_scatter | solution.py:682
  77.3 12.6 %copy-start.7 = (bf16[8,512,256]{2,1,0:T(8,128)(2,1)}, bf16[8,512,256]{2,1,0:T(8,128)(2,1)S(1)}, u32[]{:S(2)}) copy-start(bf16[8,512,256]{2,1,0:T(8,128)(2,1)S(1)} %get-tuple-element.32.kv_ref) | copy-start | bytes 6291460
  77.5 12.5 %copy-start.3 = (bf16[2,512,256]{2,1,0:T(8,128)(2,1)}, bf16[2,512,256]{2,1,0:T(8,128)(2,1)S(1)}, u32[]{:S(2)}) copy-start(bf16[2,512,256]{2,1,0:T(8,128)(2,1)S(1)} %pad_maximum_fusion.3.q_ref) | copy-start | bytes 1572868
  90.0 7.2 %copy-start.5 = (bf16[2,512,256]{2,1,0:T(8,128)(2,1)}, bf16[2,512,256]{2,1,0:T(8,128)(2,1)S(1)}, u32[]{:S(2)}) copy-start(bf16[2,512,256]{2,1,0:T(8,128)(2,1)S(1)} %get-tuple-element.33.attn_ref) | copy-start | bytes 1572868
  90.0 7.1 %collective-permute-start = (bf16[512,256]{1,0:T(8,128)(2,1)S(1)}, bf16[512,256]{1,0:T(8,128)(2,1)S(1)}, u32[]{:S(2)}, u32[]{:S(2)}) collective-permute-start(bf16[512,256]{1,0:T(8,128)(2,1)S(1)} %slice_bitcast_fusion.8), channel_id=1, source_target_pairs={{0,28},{4,24},{8,20},{12,16},{16,12},{20,8},{24,4},{28,0},{1,29},{... | collective-permute-start | bytes 786440 | tf_op jit(solution)/shard_map/ppermute | solution.py:595
  107.1 2.4 %copy-start.10 = (bf16[2048,512]{1,0:T(8,128)(2,1)}, bf16[2048,512]{1,0:T(8,128)(2,1)S(1)}, u32[]{:S(2)}) copy-start(bf16[2048,512]{1,0:T(8,128)(2,1)S(1)} %convolution_convert_fusion) | copy-start | bytes 6291460
  108.2 19.7 %collective-permute-start.2 = (bf16[4,256,512]{2,1,0:T(8,128)(2,1)}, bf16[4,256,512]{2,1,0:T(8,128)(2,1)}, u32[]{:S(2)}, u32[]{:S(2)}) collective-permute-start(bf16[4,256,512]{2,1,0:T(8,128)(2,1)} %select_bitcast_fusion), channel_id=1, source_target_pairs={{0,4},{4,0},{8,12},{12,8},{16,20},{20,16},{24,28},{28,24},{1,5},{5... | collective-permute-start | bytes 3145736 | tf_op jit(solution)/shard_map/ppermute | solution.py:602
  109.5 7.3 %copy-start.8 = (bf16[2048,512]{1,0:T(8,128)(2,1)}, bf16[2048,512]{1,0:T(8,128)(2,1)S(1)}, u32[]{:S(2)}) copy-start(bf16[2048,512]{1,0:T(8,128)(2,1)S(1)} %convolution_convert_fusion.1) | copy-start | bytes 6291460
  109.5 2.7 %copy-start.1 = (bf16[512,2048]{1,0:T(8,128)(2,1)S(1)}, bf16[512,2048]{1,0:T(8,128)(2,1)}, u32[]{:S(2)}) copy-start(bf16[512,2048]{1,0:T(8,128)(2,1)} %all-gather.2.cloned.1.call-done.refs_1_) | copy-start | bytes 6291460
  110.6 19.0 %collective-permute-start.1 = (bf16[4,256,512]{2,1,0:T(8,128)(2,1)}, bf16[4,256,512]{2,1,0:T(8,128)(2,1)}, u32[]{:S(2)}, u32[]{:S(2)}) collective-permute-start(bf16[4,256,512]{2,1,0:T(8,128)(2,1)} %select_bitcast_fusion.1), channel_id=1, source_target_pairs={{0,4},{4,0},{8,12},{12,8},{16,20},{20,16},{24,28},{28,24},{1,5},{5... | collective-permute-start | bytes 3145736 | tf_op jit(solution)/shard_map/ppermute | solution.py:602
  116.8 11.0 %copy-start.11 = (bf16[2048,512]{1,0:T(8,128)(2,1)S(1)}, bf16[2048,512]{1,0:T(8,128)(2,1)}, u32[]{:S(2)}) copy-start(bf16[2048,512]{1,0:T(8,128)(2,1)} %copy-done.10) | copy-start | bytes 6291460
  117.6 9.2 %collective-permute-start.3 = (bf16[512,256]{1,0:T(8,128)(2,1)}, bf16[512,256]{1,0:T(8,128)(2,1)}, u32[]{:S(2)}, u32[]{:S(2)}) collective-permute-start(bf16[512,256]{1,0:T(8,128)(2,1)} %get-tuple-element.78), channel_id=1, source_target_pairs={{0,28},{4,24},{8,20},{12,16},{16,12},{20,8},{24,4},{28,0},{1,29},{... | collective-permute-start | bytes 786440 | tf_op jit(solution)/shard_map/ppermute | solution.py:595
  127.8 1.9 copy-start.9
  131.5 11.0 %copy-start.4 = (bf16[2,512,256]{2,1,0:T(8,128)(2,1)S(1)}, bf16[2,512,256]{2,1,0:T(8,128)(2,1)}, u32[]{:S(2)}) copy-start(bf16[2,512,256]{2,1,0:T(8,128)(2,1)} %copy-done.3) | copy-start | bytes 1572868
  131.5 11.0 %copy-start.6 = (bf16[2,512,256]{2,1,0:T(8,128)(2,1)S(1)}, bf16[2,512,256]{2,1,0:T(8,128)(2,1)}, u32[]{:S(2)}) copy-start(bf16[2,512,256]{2,1,0:T(8,128)(2,1)} %copy-done.5) | copy-start | bytes 1572868
  131.6 10.2 %collective-permute-start.6 = (bf16[256,512]{1,0:T(8,128)(2,1)S(1)}, bf16[256,512]{1,0:T(8,128)(2,1)S(1)}, u32[]{:S(2)}, u32[]{:S(2)}) collective-permute-start(bf16[256,512]{1,0:T(8,128)(2,1)S(1)} %get-tuple-element.62), channel_id=1, source_target_pairs={{0,24},{4,28},{8,16},{12,20},{16,8},{20,12},{24,0},{28,4},{1,25},{... | collective-permute-start | bytes 786440 | tf_op jit(solution)/shard_map/ppermute | solution.py:610
  134.2 26.6 %collective-permute-start.5 = (bf16[256,512]{1,0:T(8,128)(2,1)S(1)}, bf16[256,512]{1,0:T(8,128)(2,1)S(1)}, u32[]{:S(2)}, u32[]{:S(2)}) collective-permute-start(bf16[256,512]{1,0:T(8,128)(2,1)S(1)} %get-tuple-element.63), channel_id=1, source_target_pairs={{0,16},{4,20},{8,24},{12,28},{16,0},{20,4},{24,8},{28,12},{1,17},{... | collective-permute-start | bytes 786440 | tf_op jit(solution)/shard_map/ppermute | solution.py:610
  134.2 26.6 %collective-permute-start.4 = (bf16[256,512]{1,0:T(8,128)(2,1)S(1)}, bf16[256,512]{1,0:T(8,128)(2,1)S(1)}, u32[]{:S(2)}, u32[]{:S(2)}) collective-permute-start(bf16[256,512]{1,0:T(8,128)(2,1)S(1)} %get-tuple-element.64), channel_id=1, source_target_pairs={{0,8},{4,12},{8,0},{12,4},{16,24},{20,28},{24,16},{28,20},{1,9},{5... | collective-permute-start | bytes 786440 | tf_op jit(solution)/shard_map/ppermute | solution.py:610
  135.3 25.5 %collective-permute-start.9 = (bf16[256,512]{1,0:T(8,128)(2,1)S(1)}, bf16[256,512]{1,0:T(8,128)(2,1)S(1)}, u32[]{:S(2)}, u32[]{:S(2)}) collective-permute-start(bf16[256,512]{1,0:T(8,128)(2,1)S(1)} %get-tuple-element.58), channel_id=1, source_target_pairs={{0,24},{4,28},{8,16},{12,20},{16,8},{20,12},{24,0},{28,4},{1,25},{... | collective-permute-start | bytes 786440 | tf_op jit(solution)/shard_map/ppermute | solution.py:610
  137.8 23.0 %collective-permute-start.8 = (bf16[256,512]{1,0:T(8,128)(2,1)S(1)}, bf16[256,512]{1,0:T(8,128)(2,1)S(1)}, u32[]{:S(2)}, u32[]{:S(2)}) collective-permute-start(bf16[256,512]{1,0:T(8,128)(2,1)S(1)} %get-tuple-element.59), channel_id=1, source_target_pairs={{0,16},{4,20},{8,24},{12,28},{16,0},{20,4},{24,8},{28,12},{1,17},{... | collective-permute-start | bytes 786440 | tf_op jit(solution)/shard_map/ppermute | solution.py:610
  141.8 19.0 %collective-permute-start.7 = (bf16[256,512]{1,0:T(8,128)(2,1)S(1)}, bf16[256,512]{1,0:T(8,128)(2,1)S(1)}, u32[]{:S(2)}, u32[]{:S(2)}) collective-permute-start(bf16[256,512]{1,0:T(8,128)(2,1)S(1)} %get-tuple-element.60), channel_id=1, source_target_pairs={{0,8},{4,12},{8,0},{12,4},{16,24},{20,28},{24,16},{28,20},{1,9},{5... | collective-permute-start | bytes 786440 | tf_op jit(solution)/shard_map/ppermute | solution.py:610
  (5 other events, 5.2 us)
Sparse Core Ops, SparseCore 0:
  10.2 82.4 all-gather.1
  104.3 76.7 reduce-scatter.1

commit v5 on v4

--- a/solution.py
+++ b/solution.py
@@ -262,7 +262,8 @@
     group_recv,
     local,
 ):
-    me, group = lax.axis_index("ctx"), lax.axis_index("head")
+    me = lax.axis_index("ctx")
+    group = lax.axis_index("head") * min(groups - 1, 1)
     core = lax.rem(me, 2)
     width = columns_all.shape[1] // groups
 
@@ -632,20 +633,12 @@
     )(*flat)
 
 
-def column_chunk(value, tiles, chunk):
-    width = value.shape[1] // tiles // 2
-    starts = [(2 * tile + chunk) * width for tile in range(tiles)]
-    return jnp.concatenate([value[:, start : start + width] for start in starts], 1)
-
-
 def paired_device(query_proj, projected_keys, projected_values, w_out, attended_blocks, grad_out):
     count, groups = lax.axis_size("ctx"), lax.axis_size("head")
     me = lax.axis_index("ctx")
     core, chip = lax.rem(me, 2), lax.div(me, 2)
     tokens = query_proj.shape[0]
-    own_tiles = count // groups
-    chunks = [column_chunk(grad_out, own_tiles, chunk) for chunk in range(2)]
-    last_piece = lax.all_gather(chunks[1], "head", axis=1, tiled=True)
+    piece = lax.all_gather(grad_out, "head", axis=1, tiled=True)
     key_halves, value_halves = halves_of(projected_keys), halves_of(projected_values)
 
     def own_half(halves):
@@ -661,14 +654,14 @@
         return merged_cores(terms, core, count)
 
     query_halves = halves_of(query_proj)
-    kv_all, q_other, first_piece = exchange(
+    kv_all, q_other, _ = exchange(
         True,
         0,
         count,
-        groups,
+        1,
         jnp.concatenate([key_halves, value_halves], 2),
         query_halves,
-        chunks[0],
+        query_proj[:16, :HEAD_SIZE],
     )
     q_units = jnp.stack([own_half(query_halves), q_other])
     rows = jnp.take(attended_blocks, jnp.stack([me, count - 1 - me]), axis=0)
@@ -680,24 +673,16 @@
         attn, w_out, groups, (own_columns - direct, direct)
     )
     scattered = lax.psum_scatter(scattered_terms, "head", scatter_dimension=1, tiled=True)
-    grad_attn = grad_attn_of([first_piece, last_piece], w_out, count)
-    grad_halves = halves_of(grad_attn)
+    piece, direct_terms = lax.optimization_barrier((piece, direct_terms))
+    grad_halves = halves_of(grad_attn_of([piece], w_out, count))
+    piece, grad_halves = lax.optimization_barrier((piece, grad_halves))
     grad_other = swapped(own_half(grad_halves[::-1]), count)
     g_units = jnp.stack([own_half(grad_halves), grad_other])
-    first_piece, last_piece, direct_terms = lax.optimization_barrier(
-        (first_piece, last_piece, direct_terms)
-    )
-    first_merged = weight_terms(first_piece, attn)
-    last_merged = weight_terms(last_piece, attn)
-    first_merged, last_merged, g_units = lax.optimization_barrier(
-        (first_merged, last_merged, g_units)
-    )
-    first_parts = chip_parts(first_merged, chip, count)
-    last_parts = chip_parts(last_merged, chip, count)
+    merged = weight_terms(piece, attn)
+    merged, g_units = lax.optimization_barrier((merged, g_units))
+    parts = chip_parts(merged, chip, count)
     dq_units, dkv = backward_units(rows, q_units, g_units, attn_units, totals, kv_all)
-    first_parts, last_parts, dq_units, dkv = lax.optimization_barrier(
-        (first_parts, last_parts, dq_units, dkv)
-    )
+    parts, dq_units, dkv = lax.optimization_barrier((parts, dq_units, dkv))
     dkv_all, dq_other, direct_all = exchange(
         False, 1, count, groups, dkv, dq_units, direct_terms
     )
@@ -709,9 +694,7 @@
     def kept(merged):
         return lax.dynamic_index_in_dim(merged, chip, 0, keepdims=False)
 
-    grad_wout = summed_chunks(
-        [[kept(first_merged)] + first_parts, [kept(last_merged)] + last_parts]
-    )
+    grad_wout = summed_chunks([[kept(merged)] + parts])
     grad_query = both_halves(dq_units[0], dq_other).astype(jnp.float32)
     summed = jnp.sum(
         dkv_all.reshape(count // 2, 2, tokens, 2 * HEAD_SIZE).astype(jnp.float32), 0

time: 225 us -> 191 us (0.85); the launches traced: 221 us -> 190 us
  Pallas kernels: 154 us -> 105 us
  waiting for transfers between devices: 18.4 us -> 39.5 us
    pallas_call x2, Pallas kernels: 113 us -> 63.7 us  [exchange(): pl.pallas_call(functools.partial(exchange_kernel, count, groups, spread),...]
    all_gather x1, waiting for transfers between devices: 0.02 us -> 21.3 us  [paired_device(): piece = lax.all_gather(grad_out, 'head', axis=1, tiled=True)]
    ppermute x2, starting transfers between devices: 2 us -> 5.83 us  [swapped(): lax.ppermute(value, 'ctx', [(c, count - 1 - c) for c in range(count)])]
    ppermute x6 -> x3, starting transfers between devices: 6.88 us -> 3.55 us  [chip_parts(): lax.ppermute(part, 'ctx', [(c, c ^ 2 * turn) for c in range(count)])]
    ppermute x6 -> x3, waiting for transfers between devices: 3.98 us -> 5.15 us  [chip_parts(): lax.ppermute(part, 'ctx', [(c, c ^ 2 * turn) for c in range(count)])]
  transfers between devices with their start and end apart: 12 -> 8, of which waited for: 3 -> 5; matrix products, arithmetic and copies ran while one was open for 7% -> 8% of each run, Pallas kernels for 70% -> 55%
where the time goes in v5:
time: 191 us; the launch traced here: 190 us
  Pallas kernels  105 us (55%)
  waiting for transfers between devices  39.5 us (21%)
  between operations  14.3 us (7%)
  other arithmetic  12.9 us (7%)
  starting transfers between devices  9.46 us (5%)
  local copies, waits for them, and re-layouts  5.89 us (3%)
  matrix products  2.46 us (1%)
    pallas_call x2, Pallas kernels, exchange(): pl.pallas_call(functools.partial(exchange_kernel, count, groups, spread),...  63.7 us
    all_gather x1, waiting for transfers between devices, paired_device(): piece = lax.all_gather(grad_out, 'head', axis=1, tiled=True)  21.3 us
    pallas_call x1, Pallas kernels, backward_units(): pl.pallas_call(backward_kernel, grid_spec=pltpu.PrefetchScalarGridSpec(nu...  16.9 us
    pallas_call x1, Pallas kernels, forward_units(): pl.pallas_call(forward_kernel, grid_spec=pltpu.PrefetchScalarGridSpec(num...  12.4 us
    ppermute x2, waiting for transfers between devices, swapped(): lax.ppermute(value, 'ctx', [(c, count - 1 - c) for c in range(count)])  12.4 us
    pallas_call x1, Pallas kernels, out_terms_of(): pl.pallas_call(functools.partial(out_terms_kernel, groups), out_shape=tup...  6.3 us
    ppermute x2, starting transfers between devices, swapped(): lax.ppermute(value, 'ctx', [(c, count - 1 - c) for c in range(count)])  5.83 us
    ppermute x3, waiting for transfers between devices, chip_parts(): lax.ppermute(part, 'ctx', [(c, c ^ 2 * turn) for c in range(count)])  5.15 us
  transfers between devices with their start and end apart: 8, of which 5 were waited for; matrix products, arithmetic and copies ran while one was open for 8% of the time, Pallas kernels for 55%

profile of v5, /device:TPU:0, one launch (start us, length us, event | category | flops | bytes accessed | tf_op | source)
XLA Modules:
  0.0 189.7 jit_solution(1800701821325612598)
XLA Ops:
  9.3 1.1 select_bitcast_fusion.2
  10.7 32.8 %shard_map.101 = (bf16[8,512,256]{2,1,0:T(8,128)(2,1)S(1)}, bf16[512,256]{1,0:T(8,128)(2,1)S(1)}, bf16[16,128]{1,0:T(8,128)(2,1)}) custom-call(bf16[2,512,256]{2,1,0:T(8,128)(2,1)S(1)} %maximum_maximum_fusion.blocks_ref, bf16[2,512,256]{2,1,0:T(8,128)(2,1)S(1)} %pad_maximum_fusion.1.halves_ref, bf16[16,128]{1,0:T(8,128)(2,1)S(1)} %slice.84.columns_ref), custom_call_target="tpu_custom_call" | custom-call | bytes 3145728 | tf_op jit(solution)/shard_map/pallas_call | solution.py:331
  43.7 12.4 %shard_map.102 = (bf16[2,512,256]{2,1,0:T(8,128)(2,1)S(1)}, f32[2,2,512]{2,1,0:T(2,128)S(1)}) custom-call(s32[2,8]{1,0:T(2,128)S(1)} %broadcast_select_fusion.1.rows_ref, bf16[2,512,256]{2,1,0:T(8,128)(2,1)S(1)} %pad_maximum_fusion.2.q_ref, bf16[8,512,256]{2,1,0:T(8,128)(2,1)S(1)} %get-tuple-element.28.kv_ref), custom_call_target="tpu_custom_call" | custom-call | flops 1342177280 | bytes 2097152 | tf_op jit(solution)/shard_map/pallas_call | solution.py:472
  56.2 3.3 %collective-permute-start = (bf16[512,256]{1,0:T(8,128)(2,1)S(1)}, bf16[512,256]{1,0:T(8,128)(2,1)S(1)}, u32[]{:S(2)}, u32[]{:S(2)}) collective-permute-start(bf16[512,256]{1,0:T(8,128)(2,1)S(1)} %slice_bitcast_fusion.8), channel_id=1, source_target_pairs={{0,28},{4,24},{8,20},{12,16},{16,12},{20,8},{24,4},{28,0},{1,29},{... | collective-permute-start | bytes 786440 | tf_op jit(solution)/shard_map/ppermute | solution.py:596
  59.4 6.0 %collective-permute-done = bf16[512,256]{1,0:T(8,128)(2,1)S(1)} collective-permute-done((bf16[512,256]{1,0:T(8,128)(2,1)S(1)}, bf16[512,256]{1,0:T(8,128)(2,1)S(1)}, u32[]{:S(2)}, u32[]{:S(2)}) %collective-permute-start) | collective-permute-done | bytes 262176 | tf_op jit(solution)/shard_map/ppermute | solution.py:596
  65.5 6.3 %shard_map.103 = (bf16[512,3072]{1,0:T(8,128)(2,1)}, bf16[512,1024]{1,0:T(8,128)(2,1)S(1)}) custom-call(bf16[512,512]{1,0:T(8,128)(2,1)S(1)} %pad_maximum_fusion.3.attn_ref, bf16[512,4096]{1,0:T(8,128)(2,1)} %refs_1_.1), custom_call_target="tpu_custom_call" | custom-call | flops 2147483648 | bytes 8388608 | tf_op jit(solution)/shard_map/pallas_call | solution.py:397
  71.8 21.3 %all-gather.2.cloned.1.call-done.refs_0_ = bf16[512,4096]{1,0:T(8,128)(2,1)} async-done(((bf16[512,1024]{1,0:T(8,128)(2,1)}), bf16[512,4096]{1,0:T(8,128)(2,1)}) %all-gather.2.cloned.1.call-update) | async-done | bytes 4194320 | tf_op jit(solution)/shard_map/all_gather | solution.py:641
  93.1 2.2 %copy-done.1 = bf16[512,4096]{1,0:T(8,128)(2,1)S(1)} copy-done((bf16[512,4096]{1,0:T(8,128)(2,1)S(1)}, bf16[512,4096]{1,0:T(8,128)(2,1)}, u32[]{:S(2)}) %copy-start.1) | copy-done | bytes 4194328
  95.3 4.5 %shard_map.104 = bf16[512,512]{1,0:T(8,128)(2,1)S(1)} custom-call(bf16[512,4096]{1,0:T(8,128)(2,1)S(1)} %copy-done.1, bf16[512,4096]{1,0:T(8,128)(2,1)} %refs_1_.1), custom_call_target="tpu_custom_call" | custom-call | flops 2147483648 | bytes 8388608 | tf_op jit(solution)/shard_map/pallas_call | solution.py:374
  99.9 2.5 %convolution_convert_fusion = bf16[4096,512]{1,0:T(8,128)(2,1)S(1)} fusion(bf16[512,4096]{1,0:T(8,128)(2,1)S(1)} %copy-done.1, bf16[512,256]{1,0:T(8,128)(2,1)S(1)} %get-tuple-element.60, bf16[512,256]{1,0:T(8,128)(2,1)S(1)} %get-tuple-element.59), kind=kOutput, calls=%fused_computation.1 | convolution fusion | flops 2150629376 | bytes 8912896 | tf_op jit(solution)/shard_map/dot_general | solution.py:234
  102.4 1.9 %select_bitcast_fusion = bf16[4,512,512]{2,1,0:T(8,128)(2,1)} fusion(pred[]{:T(512)S(6)} %eq.2, bf16[4,2,512,512]{3,2,1,0:T(8,128)(2,1)S(1)} %bitcast.75), kind=kLoop, calls=%fused_computation.7 | loop fusion | flops 1048576 | bytes 6291457 | tf_op jit(solution)/shard_map/jit(_where)/select_n | solution.py:602
  105.1 2.6 %collective-permute-start.2 = (bf16[512,256]{1,0:T(8,128)(2,1)S(1)}, bf16[512,256]{1,0:T(8,128)(2,1)S(1)}, u32[]{:S(2)}, u32[]{:S(2)}) collective-permute-start(bf16[512,256]{1,0:T(8,128)(2,1)S(1)} %get-tuple-element.62), channel_id=1, source_target_pairs={{0,28},{4,24},{8,20},{12,16},{16,12},{20,8},{24,4},{28,0},{1,29},{... | collective-permute-start | bytes 786440 | tf_op jit(solution)/shard_map/ppermute | solution.py:596
  107.7 6.4 %collective-permute-done.2 = bf16[512,256]{1,0:T(8,128)(2,1)S(1)} collective-permute-done((bf16[512,256]{1,0:T(8,128)(2,1)S(1)}, bf16[512,256]{1,0:T(8,128)(2,1)S(1)}, u32[]{:S(2)}, u32[]{:S(2)}) %collective-permute-start.2) | collective-permute-done | bytes 262176 | tf_op jit(solution)/shard_map/ppermute | solution.py:596
  114.1 3.8 %fusion = bf16[4,512,512]{2,1,0:T(8,128)(2,1)S(1)} fusion(bf16[4,512,512]{2,1,0:T(8,128)(2,1)} %collective-permute-done.1, pred[]{:T(512)S(6)} %eq.2, bf16[4,2,512,512]{3,2,1,0:T(8,128)(2,1)} %bitcast.76), kind=kLoop, calls=%fused_computation.4 | loop fusion | flops 5242880 | bytes 8388609 | tf_op jit(solution)/shard_map/convert_element_type | solution.py:604
  118.1 2.4 %collective-permute-start.5 = (bf16[512,512]{1,0:T(8,128)(2,1)S(1)}, bf16[512,512]{1,0:T(8,128)(2,1)S(1)}, u32[]{:S(2)}, u32[]{:S(2)}) collective-permute-start(bf16[512,512]{1,0:T(8,128)(2,1)S(1)} %get-tuple-element.50), channel_id=1, source_target_pairs={{0,24},{4,28},{8,16},{12,20},{16,8},{20,12},{24,0},{28,4},{1,25},{... | collective-permute-start | bytes 1572872 | tf_op jit(solution)/shard_map/ppermute | solution.py:611
  121.6 16.9 %shard_map.105 = (bf16[2,512,256]{2,1,0:T(8,128)(2,1)S(1)}, bf16[8,512,256]{2,1,0:T(8,128)(2,1)S(1)}) custom-call(s32[2,8]{1,0:T(2,128)S(1)} %broadcast_select_fusion.1.rows_ref, bf16[2,512,256]{2,1,0:T(8,128)(2,1)S(1)} %pad_maximum_fusion.2.q_ref, bf16[2,512,256]{2,1,0:T(8,128)(2,1)S(1)} %pad_maximum_fusion.5.g_ref, ...), custom_call_target="tpu_custom_call" | custom-call | flops 3355443200 | bytes 4194304 | tf_op jit(solution)/shard_map/pallas_call | solution.py:564
  138.5 1.3 copy-done.2
  139.9 5.1 %collective-permute-done.4.refs_2_ = bf16[512,512]{1,0:T(8,128)(2,1)S(1)} collective-permute-done((bf16[512,512]{1,0:T(8,128)(2,1)S(1)}, bf16[512,512]{1,0:T(8,128)(2,1)S(1)}, u32[]{:S(2)}, u32[]{:S(2)}) %collective-permute-start.4) | collective-permute-done | bytes 524320 | tf_op jit(solution)/shard_map/ppermute | solution.py:611
  145.0 30.9 %shard_map.106 = (bf16[8,512,256]{2,1,0:T(8,128)(2,1)S(1)}, bf16[512,256]{1,0:T(8,128)(2,1)S(1)}, bf16[512,1024]{1,0:T(8,128)(2,1)S(1)}) custom-call(bf16[8,512,256]{2,1,0:T(8,128)(2,1)} %copy-done.2, bf16[2,512,256]{2,1,0:T(8,128)(2,1)S(1)} %get-tuple-element.41.halves_ref, bf16[512,1024]{1,0:T(8,128)(2,1)S(1)} %get-tuple-element.42.columns_ref), custom_call_target="tpu_custom_call" | custom-call | bytes 9437184 | tf_op jit(solution)/shard_map/pallas_call | solution.py:331
  175.9 1.3 shard_map.107
  177.6 0.8 pad_maximum_fusion.7
  178.5 0.8 pad_maximum_fusion.6
  179.3 1.1 maximum_convert_fusion
  180.6 2.2 %pad_maximum_fusion = bf16[512,1024]{1,0:T(8,128)(2,1)} fusion(bf16[512,256]{1,0:T(8,128)(2,1)S(1)} %add_convert_fusion, bf16[512,768]{1,0:T(8,128)(2,1)} %reduce-scatter.2.cloned.1.call-done), kind=kLoop, calls=%fused_computation.8 | loop fusion | flops 2097152 | bytes 2097152 | tf_op jit(solution)/shard_map/concatenate | solution.py:692
  (45 shorter events, 5.5 us)
Async XLA Ops:
  7.2 1.6 copy-start
  7.2 3.3 %copy-start.5 = (bf16[512,256]{1,0:T(8,128)(2,1)S(1)}, bf16[512,256]{1,0:T(8,128)(2,1)}, u32[]{:S(2)}) copy-start(bf16[512,256]{1,0:T(8,128)(2,1)} %param.8) | copy-start | bytes 786436
  7.2 3.3 %copy-start.6 = (bf16[512,256]{1,0:T(8,128)(2,1)S(1)}, bf16[512,256]{1,0:T(8,128)(2,1)}, u32[]{:S(2)}) copy-start(bf16[512,256]{1,0:T(8,128)(2,1)} %param.7) | copy-start | bytes 786436
  7.2 85.9 %all-gather.2.cloned.1.call-start = ((), (), s32[]{:S(2)}) async-start(), calls=%async_computation.2 | async-start | bytes 5242880 | tf_op jit(solution)/shard_map/all_gather | solution.py:641
  7.9 172.6 %reduce-scatter.2.cloned.1.call-start = ((), (), s32[]{:S(2)}) async-start(), calls=%async_computation.1 | async-start | bytes 3932160 | tf_op jit(solution)/shard_map/reduce_scatter | solution.py:675
  43.5 12.6 %copy-start.3 = (bf16[8,512,256]{2,1,0:T(8,128)(2,1)}, bf16[8,512,256]{2,1,0:T(8,128)(2,1)S(1)}, u32[]{:S(2)}) copy-start(bf16[8,512,256]{2,1,0:T(8,128)(2,1)S(1)} %get-tuple-element.28.kv_ref) | copy-start | bytes 6291460
  56.2 9.3 %collective-permute-start = (bf16[512,256]{1,0:T(8,128)(2,1)S(1)}, bf16[512,256]{1,0:T(8,128)(2,1)S(1)}, u32[]{:S(2)}, u32[]{:S(2)}) collective-permute-start(bf16[512,256]{1,0:T(8,128)(2,1)S(1)} %slice_bitcast_fusion.8), channel_id=1, source_target_pairs={{0,28},{4,24},{8,20},{12,16},{16,12},{20,8},{24,4},{28,0},{1,29},{... | collective-permute-start | bytes 786440 | tf_op jit(solution)/shard_map/ppermute | solution.py:596
  93.1 2.2 %copy-start.1 = (bf16[512,4096]{1,0:T(8,128)(2,1)S(1)}, bf16[512,4096]{1,0:T(8,128)(2,1)}, u32[]{:S(2)}) copy-start(bf16[512,4096]{1,0:T(8,128)(2,1)} %all-gather.2.cloned.1.call-done.refs_0_) | copy-start | bytes 12582916
  102.4 2.7 %copy-start.4 = (bf16[4096,512]{1,0:T(8,128)(2,1)}, bf16[4096,512]{1,0:T(8,128)(2,1)S(1)}, u32[]{:S(2)}) copy-start(bf16[4096,512]{1,0:T(8,128)(2,1)S(1)} %convolution_convert_fusion) | copy-start | bytes 12582916
  105.1 9.0 %collective-permute-start.1 = (bf16[4,512,512]{2,1,0:T(8,128)(2,1)}, bf16[4,512,512]{2,1,0:T(8,128)(2,1)}, u32[]{:S(2)}, u32[]{:S(2)}) collective-permute-start(bf16[4,512,512]{2,1,0:T(8,128)(2,1)} %select_bitcast_fusion), channel_id=1, source_target_pairs={{0,4},{4,0},{8,12},{12,8},{16,20},{20,16},{24,28},{28,24},{1,5},{5... | collective-permute-start | bytes 6291464 | tf_op jit(solution)/shard_map/ppermute | solution.py:603
  105.1 8.9 %collective-permute-start.2 = (bf16[512,256]{1,0:T(8,128)(2,1)S(1)}, bf16[512,256]{1,0:T(8,128)(2,1)S(1)}, u32[]{:S(2)}, u32[]{:S(2)}) collective-permute-start(bf16[512,256]{1,0:T(8,128)(2,1)S(1)} %get-tuple-element.62), channel_id=1, source_target_pairs={{0,28},{4,24},{8,20},{12,16},{16,12},{20,8},{24,4},{28,0},{1,29},{... | collective-permute-start | bytes 786440 | tf_op jit(solution)/shard_map/ppermute | solution.py:596
  118.1 21.8 %collective-permute-start.5 = (bf16[512,512]{1,0:T(8,128)(2,1)S(1)}, bf16[512,512]{1,0:T(8,128)(2,1)S(1)}, u32[]{:S(2)}, u32[]{:S(2)}) collective-permute-start(bf16[512,512]{1,0:T(8,128)(2,1)S(1)} %get-tuple-element.50), channel_id=1, source_target_pairs={{0,24},{4,28},{8,16},{12,20},{16,8},{20,12},{24,0},{28,4},{1,25},{... | collective-permute-start | bytes 1572872 | tf_op jit(solution)/shard_map/ppermute | solution.py:611
  120.5 24.4 %collective-permute-start.4 = (bf16[512,512]{1,0:T(8,128)(2,1)S(1)}, bf16[512,512]{1,0:T(8,128)(2,1)S(1)}, u32[]{:S(2)}, u32[]{:S(2)}) collective-permute-start(bf16[512,512]{1,0:T(8,128)(2,1)S(1)} %get-tuple-element.51), channel_id=1, source_target_pairs={{0,16},{4,20},{8,24},{12,28},{16,0},{20,4},{24,8},{28,12},{1,17},{... | collective-permute-start | bytes 1572872 | tf_op jit(solution)/shard_map/ppermute | solution.py:611
  121.1 23.9 %collective-permute-start.3 = (bf16[512,512]{1,0:T(8,128)(2,1)S(1)}, bf16[512,512]{1,0:T(8,128)(2,1)S(1)}, u32[]{:S(2)}, u32[]{:S(2)}) collective-permute-start(bf16[512,512]{1,0:T(8,128)(2,1)S(1)} %get-tuple-element.52), channel_id=1, source_target_pairs={{0,8},{4,12},{8,0},{12,4},{16,24},{20,28},{24,16},{28,20},{1,9},{5... | collective-permute-start | bytes 1572872 | tf_op jit(solution)/shard_map/ppermute | solution.py:611
  138.5 1.3 copy-start.2
Sparse Core Ops, SparseCore 0:
  9.6 83.4 all-gather.1
  95.4 67.5 reduce-scatter.1
